TPU v7x, 32 devices: a whole 2x2x4 slice. The times are simulated.
32 devices in a mesh: slab: 8 (over z, x), grp: 4 (over y, core).
Axes of the slice: x: 2, y: 2, z: 4, core: 2. Of those that a mesh axis runs over, the one named last changes fastest.
Arguments:
- a_blocks: bfloat16 [8192, 7, 4096], P(('slab', 'grp')), may hold values from -1.5 to 1.5
- a_cols: int32 [8192, 7], P(('slab', 'grp')), may hold values from 0 to 8191, as said below
- p_blocks: bfloat16 [8192, 4096], P(('slab', 'grp')), may hold values from -0.75 to 0.75
- p_cols: int32 [8192], P(('slab', 'grp')), may hold values from 0 to 1023, as said below
- coarse_owner: int32 [32, 32], replicated, may hold values from 0 to 31, each once within a row
Outputs:
- coarse_blocks: bfloat16 [1024, 7, 4096], P(('slab', 'grp'))
Inputs may be any that keep to these rules, and one draw needn't show every extreme that they name: `a_cols`: fine block row f is the block at layer z = f // 128, y = (f // 8) mod 16, x = f mod 8; its row lists its own block and the six blocks at x +- 1 mod 8, y +- 1 mod 16, z +- 1 mod 64, each once, in any order. 8 distinct cut positions among the y values split y cyclically into 8 runs, the same in every layer and column; run = (number of cuts <= y) - 1 mod 8. The block at (z, y, x) has p_cols = (((z + 1) // 2) mod 32) * 32 + (x // 2) * 8 + run. `coarse_owner`: each row is a permutation.
All inputs are finite; a program needn't handle non-finite values.
Results may differ from a plain program's by a relative error of at most 0.0049.
Values may be sent and summed in bfloat16 or wider, within the bound.
A program may use at most 320 MiB of HBM per device.

v0:
```python
import math

import jax
import jax.numpy as jnp
from jax import lax
from jax.sharding import PartitionSpec as P

KC = 7
PX = 8
PY = 16
RUNS = 8
AXY = 32


def with_halo(x, sides, width):
    for axis, dim in sides:
        peers, length = (lax.axis_size(axis), x.shape[dim])
        up = [(i, (i + 1) % peers) for i in range(peers)]
        down = [(j, i) for i, j in up]
        last = lax.slice_in_dim(x, length - width, length, axis=dim)
        leading = lax.slice_in_dim(x, 0, width, axis=dim)
        before = lax.ppermute(last, axis, up)
        after = lax.ppermute(leading, axis, down)
        x = jnp.concatenate([before, x, after], axis=dim)
    return x


def passed_along(block, axis, distance):
    devices = range(lax.axis_size(axis))
    route = [((i - distance) % len(devices), i) for i in devices]
    return lax.ppermute(block, axis, route)


def slot_of(q_from, a_from, q_to, a_to, layer_count):
    column = q_from // RUNS
    within = q_from % RUNS
    columns = PX // 2
    left_q = (column - 1) % columns * RUNS + within
    right_q = (column + 1) % columns * RUNS + within
    down_q = column * RUNS + (within - 1) % RUNS
    upper_q = column * RUNS + (within + 1) % RUNS
    result = jnp.where(
        q_to == left_q,
        1,
        jnp.where(
            q_to == right_q, 2, jnp.where(q_to == down_q, 3, jnp.where(q_to == upper_q, 4, 0))
        ),
    )
    drift = (a_to - a_from) % layer_count
    return jnp.where(drift == 1, 6, jnp.where(drift == layer_count - 1, 5, result)).astype(
        jnp.int32
    )


def by_owner(partial_rows, owners):
    order_ids = jnp.arange(AXY, dtype=jnp.int32)
    inverse = jnp.sum(
        jnp.where(owners[None, :] == order_ids[:, None], order_ids[None, :], 0), axis=1
    )
    return partial_rows[inverse]


def per_device(a_blocks, a_cols, p_blocks, p_cols, coarse_owner):
    row_count = a_blocks.shape[0]
    stencil = a_blocks.shape[1]
    flat_width = p_blocks.shape[1]
    block_width = math.isqrt(flat_width)
    plane_size = PX * PY
    layers = lax.axis_size(("slab", "grp"))
    slab_count = lax.axis_size("slab")
    position = lax.axis_index(("slab", "grp"))
    depth_total = 2 * layers
    extended = with_halo(p_blocks.reshape(2, PY, PX, flat_width), ((("slab", "grp"), 0),), 1)
    middle = extended[1:3]
    neighbours = jnp.stack(
        [
            middle,
            jnp.roll(middle, 1, axis=2),
            jnp.roll(middle, -1, axis=2),
            jnp.roll(middle, 1, axis=1),
            jnp.roll(middle, -1, axis=1),
            extended[0:2],
            extended[2:4],
        ],
        axis=3,
    )
    neighbours = neighbours.reshape(row_count, stencil, block_width, block_width)
    depth_local = lax.broadcasted_iota(jnp.int32, (2, PY, PX), 0)
    ypos = lax.broadcasted_iota(jnp.int32, (2, PY, PX), 1)
    xpos = lax.broadcasted_iota(jnp.int32, (2, PY, PX), 2)
    depth_global = 2 * position + depth_local

    def locate(zz, yy, xx):
        return ((zz % depth_total * PY + yy % PY) * PX + xx % PX).reshape(-1)

    expected = jnp.stack(
        [
            locate(depth_global, ypos, xpos),
            locate(depth_global, ypos, xpos - 1),
            locate(depth_global, ypos, xpos + 1),
            locate(depth_global, ypos - 1, xpos),
            locate(depth_global, ypos + 1, xpos),
            locate(depth_global - 1, ypos, xpos),
            locate(depth_global + 1, ypos, xpos),
        ],
        axis=1,
    )
    stored_ids = jnp.arange(stencil, dtype=jnp.int32)
    matches = a_cols[:, None, :] == expected[:, :, None]
    chosen = jnp.sum(jnp.where(matches, stored_ids[None, None, :], 0), axis=2)
    aligned = jnp.take_along_axis(a_blocks, chosen[:, :, None], axis=1)
    aligned = aligned.reshape(row_count, stencil, block_width, block_width)
    carried = jnp.einsum(
        "fjab,fjbc->fjac", aligned, neighbours, preferred_element_type=jnp.float32
    ).astype(jnp.bfloat16)
    prolong = p_blocks.reshape(row_count, block_width, block_width)
    products = jnp.einsum("fba,fjbc->fjac", prolong, carried, preferred_element_type=jnp.float32)
    q_from = (p_cols % AXY)[:, None]
    a_from = (p_cols // AXY)[:, None]
    plane_q = p_cols[:plane_size] % AXY
    q_to = plane_q[expected % plane_size]
    a_to = (expected // plane_size + 1) // 2 % layers
    slot = slot_of(q_from, a_from, q_to, a_to, layers)
    local_layer = (a_from - position) % layers
    segment = ((local_layer * AXY + q_from) * KC + slot).reshape(-1)
    partial_value = jax.ops.segment_sum(
        products.reshape(row_count * stencil, flat_width), segment, num_segments=2 * AXY * KC
    )
    partial_value = partial_value.reshape(2, AXY, KC, flat_width)
    lower_owner = lax.dynamic_index_in_dim(coarse_owner, position, 0, keepdims=False)
    upper_owner = lax.dynamic_index_in_dim(coarse_owner, (position + 1) % layers, 0, keepdims=False)
    outgoing = jnp.stack(
        [by_owner(partial_value[0], lower_owner), by_owner(partial_value[1], upper_owner)]
    )
    outgoing = outgoing.reshape(2, slab_count, AXY // slab_count, KC, flat_width)
    arrived = lax.all_to_all(outgoing, "slab", split_axis=1, concat_axis=1, tiled=True)
    upper_part = passed_along(arrived[1], "grp", 1)
    rolled = jnp.roll(upper_part, 1, axis=0)
    upper_part = jnp.where(lax.axis_index("grp") == 0, rolled, upper_part)
    summed = arrived[0] + upper_part
    return summed.reshape(AXY, KC, flat_width).astype(jnp.bfloat16)


def solution(mesh):
    return jax.shard_map(
        per_device,
        mesh=mesh,
        in_specs=(
            P(("slab", "grp"), None, None),
            P(("slab", "grp"), None),
            P(("slab", "grp"), None),
            P(("slab", "grp")),
            P(),
        ),
        out_specs=P(("slab", "grp"), None, None),
        check_vma=False,
    )
```

profile of v0, /device:TPU:0, one launch (start us, length us, event | category | flops | bytes accessed | tf_op | source)
XLA Modules:
  0.0 700.9 jit_solution(5919122250361293064)
XLA Ops:
  0.0 3.3 slice_bitcast_fusion.2
  3.3 6.4 collective-permute-start.1
  10.0 2.6 copy.120
  12.5 2.5 fusion.64
  15.1 1.1 fusion.65
  16.2 2.6 fusion.62
  21.2 1.1 reshape.2421
  22.3 10.5 %gather_fusion = s32[1792]{0:T(1024)S(1)} fusion(s32[128]{0:T(128)S(1)} %and_select_fusion.12, s32[2048]{0:T(1024)S(1)} %pad_clamp_fusion), kind=kCustom, calls=%fused_computation | custom fusion | bytes 21504 | tf_op jit(solution)/shard_map/gather | solution.py:121
  34.6 7.4 %copy.121 = bf16[256,1,64,64]{3,2,1,0:T(8,128)(2,1)} copy(bf16[256,1,64,64]{0,3,2,1:T(8,128)(2,1)} %bitcast.100) | data formatting | bytes 4194304 | tf_op jit(solution)/shard_map/stack | solution.py:75
  42.0 5.5 constant_dynamic-update-slice_fusion
  47.5 3.4 pad_maximum_fusion.3
  51.0 6.9 stack.64
  57.8 7.2 %stack.65 = bf16[256,1,64,64]{3,2,0,1:T(8,128)(2,1)} reshape(bf16[2,16,8,4096]{3,2,1,0:T(8,128)(2,1)} %get-tuple-element.63) | data formatting | bytes 4194304 | tf_op jit(solution)/shard_map/stack | solution.py:75
  66.6 5.4 bitcast_dynamic-update-slice_fusion.5
  72.0 3.1 bitcast_dynamic-update-slice_fusion.4
  75.1 2.4 pad_maximum_fusion.5
  79.5 7.5 %copy.140 = bf16[256,64,64,1]{2,1,3,0:T(8,128)(2,1)} copy(bf16[256,64,64,1]{0,2,1,3:T(8,128)(2,1)} %bitcast.101) | data formatting | bytes 4194304 | tf_op jit(solution)/shard_map/reshape | solution.py:116
  86.9 6.9 stack.66
  93.8 6.9 stack.67
  101.0 48.5 %gather_fusion.3 = bf16[1792,4096]{1,0:T(8,128)(2,1)} fusion(bf16[256,7,4096]{2,0,1:T(8,128)(2,1)} %param.5, s32[1792]{0:T(1024)S(1)} %reshape.2443), kind=kCustom, calls=%fused_computation.3 | custom fusion | bytes 29374464 | tf_op jit(solution)/shard_map/jit(take_along_axis)/gather | solution.py:111
  149.5 40.7 %gather.17 = bf16[256,7,64,64]{3,2,1,0:T(8,128)(2,1)} reshape(bf16[1792,4096]{1,0:T(8,128)(2,1)} %gather_fusion.3) | data formatting | bytes 29360128 | tf_op jit(solution)/shard_map/jit(take_along_axis)/gather | solution.py:111
  190.5 5.4 bitcast_dynamic-update-slice_fusion.3
  195.9 3.0 bitcast_dynamic-update-slice_fusion.2
  198.9 3.9 pad_maximum_fusion.1
  202.9 7.0 %stack.68 = bf16[256,1,64,64]{3,2,0,1:T(8,128)(2,1)} reshape(bf16[2,16,8,4096]{3,2,1,0:T(8,128)(2,1)} %get-tuple-element.16) | data formatting | bytes 4194304 | tf_op jit(solution)/shard_map/stack | solution.py:75
  209.9 5.6 stack.69
  215.5 5.3 bitcast_dynamic-update-slice_fusion.1
  220.9 3.0 bitcast_dynamic-update-slice_fusion
  223.9 46.4 %fusion.5 = f32[256,7,64,64]{2,3,1,0:T(8,128)} fusion(bf16[256,64,64,1]{2,1,3,0:T(8,128)(2,1)} %copy.140, bf16[256,7,64,64]{3,2,1,0:T(8,128)(2,1)} %bitcast_dynamic-update-slice_fusion, bf16[256,7,64,64]{3,2,1,0:T(8,128)(2,1)} %gather.17, pred[256,7]{1,0:T(8,128)(4,1)S(1)} %copy.118), kind=kOutput, calls=%fused_computation.10 | convolution fusion | flops 1893728256 | bytes 60819200 | tf_op jit(solution)/shard_map/fba,fjbc->fjac/dot_general | solution.py:117
  270.3 59.6 %copy.131 = f32[256,7,64,64]{3,2,1,0:T(8,128)} copy(f32[256,7,64,64]{2,3,1,0:T(8,128)} %fusion.5) | data formatting | bytes 58720256 | tf_op jit(solution)/shard_map/fba,fjbc->fjac/transpose | solution.py:117
  329.9 47.9 %reshape.2453 = f32[1792,4096]{1,0:T(8,128)} reshape(f32[256,7,64,64]{3,2,1,0:T(8,128)} %copy.131) | data formatting | bytes 58720256 | tf_op jit(solution)/shard_map/reshape | solution.py:127
  377.8 53.7 %scatter_custom_fusion = f32[448,4096]{1,0:T(8,128)} fusion(s32[1792]{0:T(1024)S(1)} %fusion.26, f32[1792,4096]{1,0:T(8,128)} %reshape.2453, f32[]{:T(128)} %constant.268.clone.1), kind=kCustom, calls=%fused_computation.24 | custom fusion | flops 7340032 | bytes 7340544 | tf_op jit(solution)/shard_map/scatter-add | solution.py:126
  431.5 7.0 fusion.61
  438.5 3.7 squeeze.16
  442.2 5.1 gather_fusion.2
  447.3 6.4 copy.133
  453.7 3.7 squeeze.15
  457.4 5.1 gather_fusion.1
  462.5 6.5 copy.132
  469.1 5.6 pad_maximum_fusion
  474.7 163.1 %all_to_all.5 = f32[2,8,4,7,4096]{4,2,3,0,1:T(4,128)S(1)} all-to-all(f32[2,8,4,7,4096]{4,2,3,0,1:T(4,128)S(1)} %pad_maximum_fusion), channel_id=1, replica_groups=mesh['slab'=8,'grp'=4] {'slab'}, dimensions={1} | all-to-all | bytes 14680064 | tf_op jit(solution)/shard_map/all_to_all | solution.py:136
  638.2 4.0 copy.134
  642.5 42.6 %collective-permute-done.2 = f32[8,4,7,4096]{3,0,2,1:T(8,128)} collective-permute-done((f32[8,4,7,4096]{3,0,2,1:T(8,128)}, f32[8,4,7,4096]{3,0,2,1:T(8,128)}, u32[]{:S(2)}, u32[]{:S(2)}) %collective-permute-start.2) | collective-permute-done | bytes 3670048 | tf_op jit(solution)/shard_map/ppermute | solution.py:31
  685.1 4.3 copy.144
  689.3 2.6 slice.118
  692.2 5.5 fusion.15
  697.7 1.3 copy.138
  699.0 1.5 convert_element_type.11
  (100 shorter events, 9.4 us)
Async XLA Ops:
  0.0 9.9 %copy-start = (bf16[256,4096]{1,0:T(8,128)(2,1)S(1)}, bf16[256,4096]{1,0:T(8,128)(2,1)}, u32[]{:S(2)}) copy-start(bf16[256,4096]{1,0:T(8,128)(2,1)} %param.7) | copy-start | bytes 6291460
  0.0 9.7 %copy-start.13 = (s32[256]{0:T(256)S(1)}, s32[256]{0:T(256)}, u32[]{:S(2)}) copy-start(s32[256]{0:T(256)} %param.8) | copy-start | bytes 3076
  3.3 195.6 %collective-permute-start.1 = (bf16[1,16,8,4096]{3,2,1,0:T(8,128)(2,1)}, bf16[1,16,8,4096]{3,2,1,0:T(8,128)(2,1)}, u32[]{:S(2)}, u32[]{:S(2)}) collective-permute-start(bf16[1,16,8,4096]{3,2,1,0:T(8,128)(2,1)} %get-tuple-element.17), channel_id=1, source_target_pairs={{1,0},{2,1},{3,2},{4,3},{5,4},{6,5},{7,6},{8,7},{9,8},{10,9},{11,1... | collective-permute-start | bytes 3145736 | tf_op jit(solution)/shard_map/ppermute | solution.py:23
  9.7 189.2 %collective-permute-start = (bf16[1,16,8,4096]{3,2,1,0:T(8,128)(2,1)}, bf16[1,16,8,4096]{3,2,1,0:T(8,128)(2,1)}, u32[]{:S(2)}, u32[]{:S(2)}) collective-permute-start(bf16[1,16,8,4096]{3,2,1,0:T(8,128)(2,1)} %get-tuple-element.18), channel_id=1, source_target_pairs={{0,1},{1,2},{2,3},{3,4},{4,5},{5,6},{6,7},{7,8},{8,9},{9,10},{10,1... | collective-permute-start | bytes 3145736 | tf_op jit(solution)/shard_map/ppermute | solution.py:22
  16.2 4.0 copy-start.12
  42.0 5.5 copy-start.8
  42.0 5.5 copy-start.9
  66.6 5.4 copy-start.3
  72.0 3.1 copy-start.10
  72.0 3.1 copy-start.11
  190.5 5.4 copy-start.4
  202.9 7.0 %copy-start.7 = (bf16[2,16,8,4096]{3,2,1,0:T(8,128)(2,1)S(1)}, bf16[2,16,8,4096]{3,2,1,0:T(8,128)(2,1)}, u32[]{:S(2)}) copy-start(bf16[2,16,8,4096]{3,2,1,0:T(8,128)(2,1)} %get-tuple-element.15) | copy-start | bytes 6291460
  215.5 5.3 copy-start.5
  462.5 6.5 copy-start.6
  637.8 4.5 copy-start.1
  642.2 42.9 %collective-permute-start.2 = (f32[8,4,7,4096]{3,0,2,1:T(8,128)}, f32[8,4,7,4096]{3,0,2,1:T(8,128)}, u32[]{:S(2)}, u32[]{:S(2)}) collective-permute-start(f32[8,4,7,4096]{3,0,2,1:T(8,128)} %copy.134), channel_id=1, source_target_pairs={{3,0},{0,1},{1,2},{2,3},{7,4},{4,5},{5,6},{6,7},{11,8},{8,9},{9,10... | collective-permute-start | bytes 11010056 | tf_op jit(solution)/shard_map/ppermute | solution.py:31
  685.1 7.1 %copy-start.2 = (f32[2,8,4,7,4096]{4,2,3,0,1:T(4,128)S(1)}, f32[2,8,4,7,4096]{4,2,3,0,1:T(4,128)}, u32[]{:S(2)}) copy-start(f32[2,8,4,7,4096]{4,2,3,0,1:T(4,128)} %copy-done.1) | copy-start | bytes 22020100
where the time goes:
time: 712 us; the launch traced here: 701 us
  local copies, waits for them, and re-layouts  365 us (51%)
  blocking collectives  163 us (23%)
  other arithmetic  76.6 us (11%)
  matrix products  46.4 us (7%)
  waiting for transfers between devices  42.6 us (6%)
    all_to_all x1, blocking collectives, per_device(): lax.all_to_all(outgoing, 'slab', split_axis=1, concat_axis=1, tiled=True)  163 us
    gather x4, local copies, waits for them, and re-layouts, per_device(): aligned = jnp.take_along_axis(a_blocks, chosen[:, :, None], axis=1)  89.5 us
    transpose x1, local copies, waits for them, and re-layouts, per_device(): jnp.einsum('fba,fjbc->fjac', prolong, carried, preferred_element_type=jnp...  59.6 us
    scatter-add x1, other arithmetic, per_device(): jax.ops.segment_sum(products.reshape(row_count * stencil, flat_width), se...  53.7 us
    another operation x8, local copies, waits for them, and re-layouts, per_device(): jnp.stack([middle, jnp.roll(middle, 1, axis=2), jnp.roll(middle, -1, axis...  50.9 us
    reshape x1, local copies, waits for them, and re-layouts, per_device(): products.reshape(row_count * stencil, flat_width)  47.9 us
    dot_general x1, matrix products, per_device(): jnp.einsum('fba,fjbc->fjac', prolong, carried, preferred_element_type=jnp...  46.4 us
    ppermute x1, waiting for transfers between devices, passed_along(): return lax.ppermute(block, axis, route)  42.6 us
  transfers between devices with their start and end apart: 3, of which 1 were waited for; matrix products, arithmetic and copies ran while one was open for 27% of the time, Pallas kernels for 0%

commit v1 on v0

v1 whole, which is shorter than its diff:
```python
import functools

import jax
import jax.numpy as jnp
from jax import lax
from jax.experimental import pallas as pl
from jax.experimental.pallas import tpu as pltpu
from jax.sharding import PartitionSpec as P

KC = 7
PX = 8
PY = 16
RUNS = 8
AXY = 32
PLANE = PX * PY
BS = 64
HALF = BS // 2
WIDE = 2 * BS
RUN_AT = PLANE * KC
DOWN_AT = RUN_AT + PY
UP_AT = DOWN_AT + PY
PICK_AT = UP_AT + PY
F32 = jnp.float32
BF16 = jnp.bfloat16


def layer_kernel(
    out_slot, zero_slot, scal, a_ref, own_ref, zin_ref, zout_ref, out_ref,
    tmp, ptmp, vtmp, arel, prel, plhs, carried, acc,
):
    step = pl.program_id(0)
    rows = a_ref.shape[0]
    lane = lax.broadcasted_iota(jnp.int32, (HALF, WIDE), 1)
    low = lane < BS

    def swap(x):
        return pltpu.roll(x, BS, 1)

    for r in range(rows):
        for i in range(HALF):
            tmp[r, i * 8 : i * 8 + KC, :] = a_ref[r, :, i * WIDE : (i + 1) * WIDE].astype(F32)
    for r in range(rows):
        f = step * rows + r
        for j in range(KC):
            k = scal[f * KC + j]
            arel[j, f] = tmp[r, pl.ds(k, HALF, stride=8), :].astype(BF16)

    for t, ref in enumerate((own_ref, zin_ref, zout_ref)):
        for i in range(HALF):
            ptmp[t, i * rows : (i + 1) * rows, :] = ref[:, i * WIDE : (i + 1) * WIDE].astype(F32)
        for r in range(rows):
            f = step * rows + r
            val = ptmp[t, pl.ds(r, HALF, stride=rows), :]
            turned = swap(val)
            vtmp[t, r, pl.ds(0, HALF, stride=2), :] = jnp.where(low, val, turned)
            vtmp[t, r, pl.ds(1, HALF, stride=2), :] = jnp.where(low, turned, val)
            prel[t, f] = vtmp[t, r].astype(BF16)
            if t == 0:
                plhs[f // 2, r % 2, 0] = val.astype(BF16)
                plhs[f // 2, r % 2, 1] = turned.astype(BF16)

    @pl.when(step == pl.num_programs(0) - 1)
    def _():
        lane2 = lax.broadcasted_iota(jnp.int32, (BS, WIDE), 1)
        low2 = lane2 < BS

        def both(t, g):
            dup = prel[t, g].astype(F32)
            top = jnp.where(low2, dup, 0.0)
            bottom = jnp.where(low2, 0.0, dup)
            return jnp.concatenate([top, bottom], axis=0).astype(BF16)

        def carry_row(y, _):
            above = lax.rem(y + 1, PY)
            below = lax.rem(y + PY - 1, PY)
            for x in range(PX):
                g = y * PX + x
                takers = (
                    (0, g),
                    (1, y * PX + (x + 1) % PX),
                    (2, y * PX + (x - 1) % PX),
                    (3, above * PX + x),
                    (4, below * PX + x),
                )
                lhs = jnp.concatenate([arel[j, f] for j, f in takers], axis=0)
                got = jnp.dot(lhs, both(0, g), preferred_element_type=F32).astype(BF16)
                for n, (j, f) in enumerate(takers):
                    carried[j, f] = got[n * HALF : (n + 1) * HALF]
                for t in (1, 2):
                    carried[4 + t, g] = jnp.dot(
                        arel[4 + t, g], both(t, g), preferred_element_type=F32
                    ).astype(BF16)
            return 0

        lax.fori_loop(0, PY, carry_row, 0)

        acc[...] = jnp.zeros_like(acc)

        def pair(a, b):
            return jnp.concatenate(
                [jnp.where(low, a, swap(b)), jnp.where(low, swap(a), b)], axis=0
            ).astype(BF16)

        def sum_row(y, _):
            run = scal[RUN_AT + y]
            down_in = scal[DOWN_AT + y] != 0
            up_in = scal[UP_AT + y] != 0
            zero = jnp.zeros((HALF, WIDE), F32)
            for c in range(PX // 2):
                parts = ([], [], [])
                for e in range(2):
                    f = y * PX + 2 * c + e
                    own, left, right, down, up, zin, zout = (
                        carried[j, f].astype(F32) for j in range(KC)
                    )
                    inner, outer = (right, left) if e == 0 else (left, right)
                    kept = (own + inner) + zin
                    kept = kept + jnp.where(down_in, down, zero) + jnp.where(up_in, up, zero)
                    down = jnp.where(down_in, zero, down)
                    up = jnp.where(up_in, zero, up)
                    parts[0].append(pair(kept, zout))
                    parts[1].append(pair(down, up))
                    parts[2].append(pair(outer, zero) if e == 0 else pair(zero, outer))
                at = (y * PX) // 2 + c
                lhs = plhs[at].reshape(2 * BS, WIDE)[:, :BS]
                q = c * RUNS + run
                for b in range(3):
                    acc[q, b] += lax.dot_general(
                        lhs,
                        jnp.concatenate(parts[b], axis=0),
                        (((0,), (0,)), ((), ())),
                        preferred_element_type=F32,
                    )
            return 0

        lax.fori_loop(0, PY, sum_row, 0)

        slots = ((0, out_slot), (3, 4), (1, 2))

        def write_row(o, _):
            q = scal[PICK_AT + o]
            for b in range(3):
                even = acc[q, b, pl.ds(0, HALF, stride=2), :]
                odd = acc[q, b, pl.ds(1, HALF, stride=2), :]
                tmp[0, pl.ds(slots[b][0], HALF, stride=8), :] = jnp.where(low, even, swap(odd))
                tmp[0, pl.ds(slots[b][1], HALF, stride=8), :] = jnp.where(low, swap(even), odd)
            tmp[0, pl.ds(zero_slot, HALF, stride=8), :] = jnp.zeros((HALF, WIDE), F32)
            for i in range(HALF):
                out_ref[o, :, i * WIDE : (i + 1) * WIDE] = tmp[0, i * 8 : i * 8 + KC, :].astype(
                    out_ref.dtype
                )
            return 0

        lax.fori_loop(0, AXY, write_row, 0)


def layer_part(a_blocks, layer, scalars, own, zin, zout, out_slot, zero_slot, dtype):
    rows = 16
    steps = PLANE // rows
    flat = BS * BS
    plane_spec = pl.BlockSpec((rows, flat), lambda s, _: (s, 0))
    return pl.pallas_call(
        functools.partial(layer_kernel, out_slot, zero_slot),
        out_shape=jax.ShapeDtypeStruct((AXY, KC, flat), dtype),
        grid_spec=pltpu.PrefetchScalarGridSpec(
            num_scalar_prefetch=1,
            grid=(steps,),
            in_specs=[
                pl.BlockSpec((rows, KC, flat), lambda s, _: (layer * steps + s, 0, 0)),
                plane_spec,
                plane_spec,
                plane_spec,
            ],
            out_specs=pl.BlockSpec((AXY, KC, flat), lambda s, _: (0, 0, 0)),
            scratch_shapes=[
                pltpu.VMEM((rows, 8 * HALF, WIDE), F32),
                pltpu.VMEM((3, rows * HALF, WIDE), F32),
                pltpu.VMEM((3, rows, BS, WIDE), F32),
                pltpu.VMEM((KC, PLANE, HALF, WIDE), BF16),
                pltpu.VMEM((3, PLANE, BS, WIDE), BF16),
                pltpu.VMEM((PLANE // 2, 2, 2, HALF, WIDE), BF16),
                pltpu.VMEM((KC, PLANE, HALF, WIDE), BF16),
                pltpu.VMEM((AXY, 3, BS, WIDE), F32),
            ],
        ),
        compiler_params=pltpu.CompilerParams(vmem_limit_bytes=56 * 1024 * 1024),
        cost_estimate=pl.CostEstimate(
            flops=PLANE * KC * 4 * BS**3,
            bytes_accessed=PLANE * KC * flat * 2,
            transcendentals=0,
        ),
        name="layer_" + ("upper" if layer else "lower"),
    )(scalars, a_blocks, own, zin, zout)


def per_device(a_blocks, a_cols, p_blocks, p_cols, coarse_owner):
    axes = ("slab", "grp")
    layers = lax.axis_size(axes)
    position = lax.axis_index(axes)
    depth_total = 2 * layers
    up = [(i, (i + 1) % layers) for i in range(layers)]
    down = [(j, i) for i, j in up]
    plane0 = p_blocks[:PLANE]
    plane1 = p_blocks[PLANE:]
    after = lax.ppermute(plane0, axes, down)
    before = lax.ppermute(plane1, axes, up)

    depth = 2 * position + lax.broadcasted_iota(jnp.int32, (2, PY, PX), 0)
    ypos = lax.broadcasted_iota(jnp.int32, (2, PY, PX), 1)
    xpos = lax.broadcasted_iota(jnp.int32, (2, PY, PX), 2)

    def locate(zz, yy, xx):
        return ((zz % depth_total * PY + yy % PY) * PX + xx % PX).reshape(2, PLANE)

    beside = [
        locate(depth, ypos, xpos),
        locate(depth, ypos, xpos - 1),
        locate(depth, ypos, xpos + 1),
        locate(depth, ypos - 1, xpos),
        locate(depth, ypos + 1, xpos),
    ]
    below, over = locate(depth - 1, ypos, xpos), locate(depth + 1, ypos, xpos)
    beside.append(jnp.stack([below[0], over[1]]))
    beside.append(jnp.stack([over[0], below[1]]))
    expected = jnp.stack(beside, axis=2)
    matches = a_cols.reshape(2, PLANE, 1, KC) == expected[..., None]
    chosen = jnp.sum(jnp.where(matches, jnp.arange(KC, dtype=jnp.int32), 0), axis=3)

    runs = p_cols[:PLANE].reshape(PY, PX)[:, 0] % RUNS
    down_in = (jnp.roll(runs, 1) == runs).astype(jnp.int32)
    up_in = (jnp.roll(runs, -1) == runs).astype(jnp.int32)

    def scalars(layer):
        owners = lax.dynamic_index_in_dim(
            coarse_owner, (position + layer) % layers, 0, keepdims=False
        )
        order = jnp.arange(AXY, dtype=jnp.int32)
        picked = jnp.sum(jnp.where(owners[None, :] == order[:, None], order[None, :], 0), axis=1)
        return jnp.concatenate([chosen[layer].reshape(-1), runs, down_in, up_in, picked])

    upper = layer_part(a_blocks, 1, scalars(1), plane1, after, plane0, 5, 6, BF16)
    arrived = lax.ppermute(upper, axes, up)
    lower = layer_part(a_blocks, 0, scalars(0), plane0, before, plane1, 6, 5, F32)
    summed = (lower + arrived.astype(F32)).astype(BF16)
    return lax.all_to_all(summed, "slab", split_axis=0, concat_axis=0, tiled=True)


def solution(mesh):
    return jax.shard_map(
        per_device,
        mesh=mesh,
        in_specs=(
            P(("slab", "grp"), None, None),
            P(("slab", "grp"), None),
            P(("slab", "grp"), None),
            P(("slab", "grp")),
            P(),
        ),
        out_specs=P(("slab", "grp"), None, None),
        check_vma=False,
    )
```

time: 712 us -> 185 us (0.26); the launches traced: 701 us -> 183 us
  local copies, waits for them, and re-layouts: 365 us -> 32.7 us
  blocking collectives: 163 us -> 44.5 us
  other arithmetic: 76.6 us -> 6.11 us
  Pallas kernels: 0 us -> 56.5 us
  matrix products: 46.4 us -> 0 us
    all_to_all x1, blocking collectives: 163 us -> 44.5 us  [per_device(): lax.all_to_all(summed, 'slab', split_axis=0, concat_axis=0, tiled=True)]
    gather x9 -> x0, local copies, waits for them, and re-layouts: 112 us -> none  [the longest x4 89.5 us: per_device(): aligned = jnp.take_along_axis(a_blocks, chosen[:, :, None], axis=1)]
    another operation x14 -> x2, local copies, waits for them, and re-layouts: 64.2 us -> 0.4 us  [scalars(): chosen[layer].reshape(-1)]
    transpose x1 -> x0, local copies, waits for them, and re-layouts: 59.6 us -> none  [per_device(): jnp.einsum('fba,fjbc->fjac', prolong, carried, preferred_element_type=jnp...]
    pallas_call x0 -> x2, Pallas kernels: none -> 56.5 us  [layer_part(): pl.pallas_call(functools.partial(layer_kernel, out_slot, zero_slot), out_...]
    reshape x2 -> x1, local copies, waits for them, and re-layouts: 55.4 us -> 0.08 us  [per_device(): runs = p_cols[:PLANE].reshape(PY, PX)[:, 0] % RUNS]
    scatter-add x1 -> x0, other arithmetic: 53.7 us -> none  [per_device(): jax.ops.segment_sum(products.reshape(row_count * stencil, flat_width), se...]
    dot_general x1 -> x0, matrix products: 46.4 us -> none  [per_device(): jnp.einsum('fba,fjbc->fjac', prolong, carried, preferred_element_type=jnp...]
  transfers between devices with their start and end apart: 3 -> 3, of which waited for: 1 -> 1; matrix products, arithmetic and copies ran while one was open for 27% -> 14% of each run, Pallas kernels for 0% -> 16%
where the time goes in v1:
time: 185 us; the launch traced here: 183 us
  Pallas kernels  56.5 us (31%)
  blocking collectives  44.5 us (24%)
  waiting for transfers between devices  36.4 us (20%)
  local copies, waits for them, and re-layouts  32.7 us (18%)
  starting transfers between devices  6.49 us (4%)
  other arithmetic  6.11 us (3%)
    pallas_call x2, Pallas kernels, layer_part(): pl.pallas_call(functools.partial(layer_kernel, out_slot, zero_slot), out_...  56.5 us
    all_to_all x1, blocking collectives, per_device(): lax.all_to_all(summed, 'slab', split_axis=0, concat_axis=0, tiled=True)  44.5 us
    ppermute x1, waiting for transfers between devices, per_device(): before = lax.ppermute(plane1, axes, up)  36.4 us
    unnamed x9, local copies, waits for them, and re-layouts  18.4 us
    ppermute x1, starting transfers between devices, per_device(): after = lax.ppermute(plane0, axes, down)  6.37 us
    convert_element_type x1, other arithmetic, per_device(): summed = (lower + arrived.astype(F32)).astype(BF16)  4 us
  transfers between devices with their start and end apart: 3, of which 1 were waited for; matrix products, arithmetic and copies ran while one was open for 14% of the time, Pallas kernels for 16%

profile of v1, /device:TPU:0, one launch (start us, length us, event | category | flops | bytes accessed | tf_op | source)
XLA Modules:
  0.0 183.1 jit_solution(16862573121125383085)
XLA Ops:
  0.0 2.8 %fusion.11 = (bf16[128,4096]{1,0:T(8,128)(2,1)}, bf16[128,4096]{1,0:T(8,128)(2,1)S(1)}) fusion(bf16[256,4096]{1,0:T(8,128)(2,1)} %param.7), kind=kLoop, calls=%fused_computation.78 | loop fusion | bytes 4194304 | tf_op jit(solution)/shard_map/slice | solution.py:204
  2.8 6.4 %collective-permute-start.1 = (bf16[128,4096]{1,0:T(8,128)(2,1)S(1)}, bf16[128,4096]{1,0:T(8,128)(2,1)S(1)}, u32[]{:S(2)}, u32[]{:S(2)}) collective-permute-start(bf16[128,4096]{1,0:T(8,128)(2,1)S(1)} %get-tuple-element.8.own_ref.zout_ref), channel_id=1, source_target_pairs={{1,0},{2,1},{3,2},{4,3},{5,4},{6,5},{7,6},{8,7},{9,8},{10,9},{11,1... | collective-permute-start | bytes 3145736 | tf_op jit(solution)/shard_map/ppermute | solution.py:205
  9.3 0.1 iota.229
  9.4 0.1 iota.232
  9.5 0.1 and.143
  9.7 0.1 iota.220
  9.9 0.1 iota.223
  10.0 0.1 and.141
  10.2 0.1 iota.238
  10.3 0.1 iota.241
  10.4 0.1 and.145
  10.5 0.1 iota.247
  10.6 0.1 iota.250
  10.7 0.1 and.147
  10.8 0.1 iota.256
  11.0 0.1 iota.259
  11.2 0.1 and.149
  11.3 0.1 iota.265
  11.5 0.1 iota.268
  11.7 0.1 and.151
  11.8 0.1 select_add_fusion.1
  11.9 0.1 slice.67
  12.0 0.1 slice.69
  12.1 0.1 slice.71
  12.2 0.1 slice.73
  12.4 0.1 constant_dynamic-update-slice_fusion.3
  12.5 0.1 constant_dynamic-update-slice_fusion.2
  12.6 0.8 dynamic-slice_bitcast_fusion
  13.4 0.1 copy.25
  13.5 0.2 reshape_squeeze.7
  13.8 17.4 %copy.24.a_ref = bf16[256,7,4096]{2,1,0:T(8,128)(2,1)} copy(bf16[256,7,4096]{2,0,1:T(8,128)(2,1)} %param.5) | data formatting | bytes 29360128 | tf_op args[0]
  31.2 0.1 slice_reduce_fusion
  31.4 0.7 fusion.16
  32.0 0.1 select_reduce_fusion
  32.2 1.3 compare_convert_fusion
  33.5 0.7 concatenate.17.scal
  34.2 1.0 copy-done.2
  35.2 28.0 %layer_upper.1 = bf16[32,7,4096]{2,1,0:T(8,128)(2,1)} custom-call(s32[976]{0:T(1024)} %concatenate.17.scal, bf16[256,7,4096]{2,1,0:T(8,128)(2,1)} %copy.24.a_ref, bf16[128,4096]{1,0:T(8,128)(2,1)} %get-tuple-element.7.zout_ref.own_ref, bf16[128,4096]{1,0:T(8,128)(2,1)} %copy-done.2, bf16[128,4096]{1,0:T(8,128)(2,1)} %copy-done.1), custom_call_target="tpu_custom_call" | custom-call | flops 939524096 | bytes 7340032 | tf_op jit(solution)/shard_map/layer_upper/pallas_call | solution.py:162
  63.2 2.8 %copy.27 = bf16[32,7,4096]{2,0,1:T(8,128)(2,1)S(1)} copy(bf16[32,7,4096]{2,1,0:T(8,128)(2,1)} %layer_upper.1) | data formatting | bytes 3670016 | tf_op jit(solution)/shard_map/layer_upper/pallas_call | solution.py:162
  66.2 0.1 copy.23
  66.3 0.2 reshape_squeeze.6
  66.5 0.1 select_reduce_fusion.1
  66.6 0.7 concatenate.16.scal
  67.3 36.4 %collective-permute-done.zin_ref = bf16[128,4096]{1,0:T(8,128)(2,1)} collective-permute-done((bf16[128,4096]{1,0:T(8,128)(2,1)S(1)}, bf16[128,4096]{1,0:T(8,128)(2,1)}, u32[]{:S(2)}, u32[]{:S(2)}) %collective-permute-start) | collective-permute-done | bytes 1048608 | tf_op jit(solution)/shard_map/ppermute | solution.py:206
  103.7 28.5 %layer_lower.1 = f32[32,7,4096]{2,1,0:T(8,128)} custom-call(s32[976]{0:T(1024)} %concatenate.16.scal, bf16[256,7,4096]{2,1,0:T(8,128)(2,1)} %copy.24.a_ref, bf16[128,4096]{1,0:T(8,128)(2,1)} %copy-done.1, bf16[128,4096]{1,0:T(8,128)(2,1)} %collective-permute-done.zin_ref, bf16[128,4096]{1,0:T(8,128)(2,1)} %get-tuple-element.7.zout_ref.own_ref), custom_call_target="tpu_custom_call" | custom-call | flops 939524096 | bytes 7340032 | tf_op jit(solution)/shard_map/layer_lower/pallas_call | solution.py:162
  132.2 4.0 %add_convert_fusion = bf16[32,7,4096]{2,1,0:T(8,128)(2,1)S(1)} fusion(f32[32,7,4096]{2,1,0:T(8,128)} %layer_lower.1, bf16[32,7,4096]{2,0,1:T(8,128)(2,1)} %collective-permute-done.2), kind=kLoop, calls=%fused_computation | loop fusion | flops 2752512 | bytes 7340032 | tf_op jit(solution)/shard_map/convert_element_type | solution.py:244
  136.2 44.5 %all_to_all.5 = bf16[32,7,4096]{2,1,0:T(8,128)(2,1)S(1)} all-to-all(bf16[32,7,4096]{2,1,0:T(8,128)(2,1)S(1)} %add_convert_fusion), channel_id=1, replica_groups=mesh['slab'=8,'grp'=4] {'slab'}, dimensions={0} | all-to-all | bytes 3670016 | tf_op jit(solution)/shard_map/all_to_all | solution.py:245
  180.7 2.4 %copy.29 = bf16[32,7,4096]{2,0,1:T(8,128)(2,1)} copy(bf16[32,7,4096]{2,1,0:T(8,128)(2,1)S(1)} %all_to_all.5) | data formatting | bytes 3670016 | tf_op jit(solution)/shard_map/all_to_all | solution.py:245
  (59 shorter events, 1.3 us)
Async XLA Ops:
  0.0 12.2 %copy-start.3 = (s32[256,7]{0,1:T(8,128)S(1)}, s32[256,7]{0,1:T(8,128)}, u32[]{:S(2)}) copy-start(s32[256,7]{0,1:T(8,128)} %param.6) | copy-start | bytes 21508
  0.0 13.7 %slice-start = ((s32[256]{0:T(256)}), s32[128]{0:T(128)S(1)}, s32[]{:S(2)}) async-start(s32[256]{0:T(256)} %param.8), calls=%async_computation.1 | async-start | bytes 1024 | tf_op jit(solution)/shard_map/slice | solution.py:229
  2.8 28.5 %copy-start.1 = (bf16[128,4096]{1,0:T(8,128)(2,1)}, bf16[128,4096]{1,0:T(8,128)(2,1)S(1)}, u32[]{:S(2)}) copy-start(bf16[128,4096]{1,0:T(8,128)(2,1)S(1)} %get-tuple-element.8.own_ref.zout_ref) | copy-start | bytes 3145732
  2.8 31.4 %collective-permute-start.1 = (bf16[128,4096]{1,0:T(8,128)(2,1)S(1)}, bf16[128,4096]{1,0:T(8,128)(2,1)S(1)}, u32[]{:S(2)}, u32[]{:S(2)}) collective-permute-start(bf16[128,4096]{1,0:T(8,128)(2,1)S(1)} %get-tuple-element.8.own_ref.zout_ref), channel_id=1, source_target_pairs={{1,0},{2,1},{3,2},{4,3},{5,4},{6,5},{7,6},{8,7},{9,8},{10,9},{11,1... | collective-permute-start | bytes 3145736 | tf_op jit(solution)/shard_map/ppermute | solution.py:205
  34.2 1.0 copy-start.2
  63.2 2.9 %copy-start = (bf16[128,4096]{1,0:T(8,128)(2,1)S(1)}, bf16[128,4096]{1,0:T(8,128)(2,1)}, u32[]{:S(2)}) copy-start(bf16[128,4096]{1,0:T(8,128)(2,1)} %get-tuple-element.7.zout_ref.own_ref) | copy-start | bytes 3145732
  66.0 66.2 %collective-permute-start.2 = (bf16[32,7,4096]{2,0,1:T(8,128)(2,1)S(1)}, bf16[32,7,4096]{2,0,1:T(8,128)(2,1)}, u32[]{:S(2)}, u32[]{:S(2)}) collective-permute-start(bf16[32,7,4096]{2,0,1:T(8,128)(2,1)S(1)} %copy.27), channel_id=1, source_target_pairs={{0,1},{1,2},{2,3},{3,4},{4,5},{5,6},{6,7},{7,8},{8,9},{9,10},{10,1... | collective-permute-start | bytes 5505032 | tf_op jit(solution)/shard_map/ppermute | solution.py:242
  66.1 37.6 %collective-permute-start = (bf16[128,4096]{1,0:T(8,128)(2,1)S(1)}, bf16[128,4096]{1,0:T(8,128)(2,1)}, u32[]{:S(2)}, u32[]{:S(2)}) collective-permute-start(bf16[128,4096]{1,0:T(8,128)(2,1)S(1)} %copy-done), channel_id=1, source_target_pairs={{0,1},{1,2},{2,3},{3,4},{4,5},{5,6},{6,7},{7,8},{8,9},{9,10},{10,1... | collective-permute-start | bytes 3145736 | tf_op jit(solution)/shard_map/ppermute | solution.py:206

commit v2 on v1

v2 whole, which is shorter than its diff:
```python
import functools

import jax
import jax.numpy as jnp
from jax import lax
from jax.experimental import pallas as pl
from jax.experimental.pallas import tpu as pltpu
from jax.sharding import PartitionSpec as P

KC = 7
PX = 8
PY = 16
RUNS = 8
AXY = 32
PLANE = PX * PY
BS = 64
HALF = BS // 2
WIDE = 2 * BS
F32 = jnp.float32
BF16 = jnp.bfloat16


def swap(x):
    return pltpu.roll(x, BS, 1)


def spread(val, low, store):
    turned = swap(val)
    store[pl.ds(0, HALF, stride=2), :] = jnp.where(low, val, turned)
    store[pl.ds(1, HALF, stride=2), :] = jnp.where(low, turned, val)
    return turned


def align_kernel(scal, a_ref, p_ref, arel, prel, plhs, tmp, vtmp):
    step = pl.program_id(0)
    rows = a_ref.shape[1]
    low = lax.broadcasted_iota(jnp.int32, (HALF, WIDE), 1) < BS
    for k in range(KC):
        for i in range(HALF):
            tmp[k, i * rows : (i + 1) * rows, :] = a_ref[k, :, i * WIDE : (i + 1) * WIDE].astype(F32)
    for i in range(HALF):
        tmp[KC, i * rows : (i + 1) * rows, :] = p_ref[:, i * WIDE : (i + 1) * WIDE].astype(F32)
    for r in range(rows):
        for j in range(KC):
            k = scal[(step * rows + r) * KC + j]
            arel[j, r] = tmp[k, pl.ds(r, HALF, stride=rows), :].astype(BF16)
        val = tmp[KC, pl.ds(r, HALF, stride=rows), :]
        turned = spread(val, low, vtmp.at[r])
        prel[r] = vtmp[r].astype(BF16)
        plhs[r // 2, r % 2, 0] = val.astype(BF16)
        plhs[r // 2, r % 2, 1] = turned.astype(BF16)


def aligned(a_blocks, p_blocks, chosen):
    rows = 16
    count, flat = p_blocks.shape
    return pl.pallas_call(
        align_kernel,
        out_shape=(
            jax.ShapeDtypeStruct((KC, count, HALF, WIDE), BF16),
            jax.ShapeDtypeStruct((count, BS, WIDE), BF16),
            jax.ShapeDtypeStruct((count // 2, 2, 2, HALF, WIDE), BF16),
        ),
        grid_spec=pltpu.PrefetchScalarGridSpec(
            num_scalar_prefetch=1,
            grid=(count // rows,),
            in_specs=[
                pl.BlockSpec((KC, rows, flat), lambda s, _: (0, s, 0)),
                pl.BlockSpec((rows, flat), lambda s, _: (s, 0)),
            ],
            out_specs=(
                pl.BlockSpec((KC, rows, HALF, WIDE), lambda s, _: (0, s, 0, 0)),
                pl.BlockSpec((rows, BS, WIDE), lambda s, _: (s, 0, 0)),
                pl.BlockSpec((rows // 2, 2, 2, HALF, WIDE), lambda s, _: (s, 0, 0, 0, 0)),
            ),
            scratch_shapes=[
                pltpu.VMEM((KC + 1, rows * HALF, WIDE), F32),
                pltpu.VMEM((rows, BS, WIDE), F32),
            ],
        ),
        compiler_params=pltpu.CompilerParams(vmem_limit_bytes=32 * 1024 * 1024),
        cost_estimate=pl.CostEstimate(
            flops=0, bytes_accessed=5 * KC * count * flat, transcendentals=0
        ),
        name="align_blocks",
    )(chosen, a_blocks, p_blocks)


def layer_kernel(
    out_slot, zero_slot, scal, a_plane, a_down, a_up, a_zin, a_zout, p_own, p_out, zin_ref, plhs,
    out_ref, ptmp, vtmp, pin, carried, acc,
):
    y = pl.program_id(0)
    low = lax.broadcasted_iota(jnp.int32, (HALF, WIDE), 1) < BS
    low2 = lax.broadcasted_iota(jnp.int32, (BS, WIDE), 1) < BS

    @pl.when(y == 0)
    def _():
        rows = 16

        def some(n, _):
            part = zin_ref[pl.ds(pl.multiple_of(n * rows, rows), rows), :]
            for i in range(HALF):
                ptmp[i * rows : (i + 1) * rows, :] = part[:, i * WIDE : (i + 1) * WIDE].astype(F32)
            for r in range(rows):
                spread(ptmp[pl.ds(r, HALF, stride=rows), :], low, vtmp.at[r])
                pin[n * rows + r] = vtmp[r].astype(BF16)
            return 0

        lax.fori_loop(0, PLANE // rows, some, 0)

    def both(block):
        dup = block.astype(F32)
        top = jnp.where(low2, dup, 0.0)
        bottom = jnp.where(low2, 0.0, dup)
        return jnp.concatenate([top, bottom], axis=0).astype(BF16)

    above = lax.rem(y + 1, PY)
    below = lax.rem(y + PY - 1, PY)
    for x in range(PX):
        g = y * PX + x
        after, before = (x + 1) % PX, (x - 1) % PX
        lhs = jnp.concatenate(
            [a_plane[0, x], a_plane[1, after], a_plane[2, before], a_down[0, x], a_up[0, x]], axis=0
        )
        takers = (g, y * PX + after, y * PX + before, above * PX + x, below * PX + x)
        got = jnp.dot(lhs, both(p_own[x]), preferred_element_type=F32).astype(BF16)
        for j, f in enumerate(takers):
            carried[j, f] = got[j * HALF : (j + 1) * HALF]
        carried[5, g] = jnp.dot(a_zin[0, x], both(pin[g]), preferred_element_type=F32).astype(BF16)
        carried[6, g] = jnp.dot(a_zout[0, x], both(p_out[x]), preferred_element_type=F32).astype(
            BF16
        )

    @pl.when(y == pl.num_programs(0) - 1)
    def _():
        acc[...] = jnp.zeros_like(acc)

        def pair(a, b):
            return jnp.concatenate(
                [jnp.where(low, a, swap(b)), jnp.where(low, swap(a), b)], axis=0
            ).astype(BF16)

        def sum_row(y, _):
            run = scal[y]
            down_in = scal[PY + y] != 0
            up_in = scal[2 * PY + y] != 0
            zero = jnp.zeros((HALF, WIDE), F32)
            for c in range(PX // 2):
                parts = ([], [], [])
                for e in range(2):
                    f = y * PX + 2 * c + e
                    own, left, right, down, up, zin, zout = (
                        carried[j, f].astype(F32) for j in range(KC)
                    )
                    inner, outer = (right, left) if e == 0 else (left, right)
                    kept = (own + inner) + zin
                    kept = kept + jnp.where(down_in, down, zero) + jnp.where(up_in, up, zero)
                    down = jnp.where(down_in, zero, down)
                    up = jnp.where(up_in, zero, up)
                    parts[0].append(pair(kept, zout))
                    parts[1].append(pair(down, up))
                    parts[2].append(pair(outer, zero) if e == 0 else pair(zero, outer))
                at = (y * PX) // 2 + c
                lhs = plhs[at].reshape(2 * BS, WIDE)[:, :BS]
                q = c * RUNS + run
                for b in range(3):
                    acc[q, b] += lax.dot_general(
                        lhs,
                        jnp.concatenate(parts[b], axis=0),
                        (((0,), (0,)), ((), ())),
                        preferred_element_type=F32,
                    )
            return 0

        lax.fori_loop(0, PY, sum_row, 0)

        slots = ((0, out_slot), (3, 4), (1, 2))

        def write_row(o, _):
            q = scal[3 * PY + o]
            for b in range(3):
                even = acc[q, b, pl.ds(0, HALF, stride=2), :]
                odd = acc[q, b, pl.ds(1, HALF, stride=2), :]
                out_ref[o, slots[b][0]] = jnp.where(low, even, swap(odd)).astype(out_ref.dtype)
                out_ref[o, slots[b][1]] = jnp.where(low, swap(even), odd).astype(out_ref.dtype)
            out_ref[o, zero_slot] = jnp.zeros((HALF, WIDE), out_ref.dtype)
            return 0

        lax.fori_loop(0, AXY, write_row, 0)


def layer_part(blocks, layer, scalars, zin, out_slot, zero_slot, dtype):
    arel, prel, plhs = blocks
    flat = BS * BS
    base = layer * PY
    other = (1 - layer) * PY

    def taken(first, count, shift):
        return pl.BlockSpec(
            (count, PX, HALF, WIDE),
            lambda y, _: (first // count, base + lax.rem(y + PY + shift, PY), 0, 0),
        )

    return pl.pallas_call(
        functools.partial(layer_kernel, out_slot, zero_slot),
        out_shape=jax.ShapeDtypeStruct((AXY, KC, HALF, WIDE), dtype),
        grid_spec=pltpu.PrefetchScalarGridSpec(
            num_scalar_prefetch=1,
            grid=(PY,),
            in_specs=[
                taken(0, 3, 0),
                taken(3, 1, 1),
                taken(4, 1, -1),
                taken(5, 1, 0),
                taken(6, 1, 0),
                pl.BlockSpec((PX, BS, WIDE), lambda y, _: (base + y, 0, 0)),
                pl.BlockSpec((PX, BS, WIDE), lambda y, _: (other + y, 0, 0)),
                pl.BlockSpec((PLANE, flat), lambda y, _: (0, 0)),
                pl.BlockSpec((PLANE // 2, 2, 2, HALF, WIDE), lambda y, _: (layer, 0, 0, 0, 0)),
            ],
            out_specs=pl.BlockSpec((AXY, KC, HALF, WIDE), lambda y, _: (0, 0, 0, 0)),
            scratch_shapes=[
                pltpu.VMEM((16 * HALF, WIDE), F32),
                pltpu.VMEM((16, BS, WIDE), F32),
                pltpu.VMEM((PLANE, BS, WIDE), BF16),
                pltpu.VMEM((KC, PLANE, HALF, WIDE), BF16),
                pltpu.VMEM((AXY, 3, BS, WIDE), F32),
            ],
        ),
        compiler_params=pltpu.CompilerParams(vmem_limit_bytes=48 * 1024 * 1024),
        cost_estimate=pl.CostEstimate(
            flops=PLANE * KC * 4 * BS**3,
            bytes_accessed=PLANE * KC * flat * 2,
            transcendentals=0,
        ),
        name="layer_" + ("upper" if layer else "lower"),
    )(scalars, arel, arel, arel, arel, arel, prel, prel, zin, plhs)


def flat_kernel(in_ref, out_ref, tmp):
    rows = in_ref.shape[0]
    tmp[...] = in_ref[:, 0].astype(F32).reshape(rows * HALF, WIDE)
    for i in range(HALF):
        out_ref[0, :, i * WIDE : (i + 1) * WIDE] = tmp[pl.ds(i, rows, stride=HALF), :].astype(BF16)


def flattened(blocks):
    rows = blocks.shape[0]
    flat = BS * BS
    return pl.pallas_call(
        flat_kernel,
        out_shape=jax.ShapeDtypeStruct((KC, rows, flat), BF16),
        grid=(KC,),
        in_specs=[pl.BlockSpec((rows, 1, HALF, WIDE), lambda s: (0, s, 0, 0))],
        out_specs=pl.BlockSpec((1, rows, flat), lambda s: (s, 0, 0)),
        scratch_shapes=[pltpu.VMEM((rows * HALF, WIDE), F32)],
        name="flatten_rows",
    )(blocks)


def per_device(a_blocks, a_cols, p_blocks, p_cols, coarse_owner):
    axes = ("slab", "grp")
    layers = lax.axis_size(axes)
    position = lax.axis_index(axes)
    depth_total = 2 * layers
    up = [(i, (i + 1) % layers) for i in range(layers)]
    down = [(j, i) for i, j in up]
    plane0 = p_blocks[:PLANE]
    plane1 = p_blocks[PLANE:]
    after = lax.ppermute(plane0, axes, down)
    before = lax.ppermute(plane1, axes, up)
    after, before = lax.optimization_barrier((after, before))

    depth = 2 * position + lax.broadcasted_iota(jnp.int32, (2, PY, PX), 0)
    ypos = lax.broadcasted_iota(jnp.int32, (2, PY, PX), 1)
    xpos = lax.broadcasted_iota(jnp.int32, (2, PY, PX), 2)

    def locate(zz, yy, xx):
        return ((zz % depth_total * PY + yy % PY) * PX + xx % PX).reshape(2, PLANE)

    beside = [
        locate(depth, ypos, xpos),
        locate(depth, ypos, xpos - 1),
        locate(depth, ypos, xpos + 1),
        locate(depth, ypos - 1, xpos),
        locate(depth, ypos + 1, xpos),
    ]
    below, over = locate(depth - 1, ypos, xpos), locate(depth + 1, ypos, xpos)
    beside.append(jnp.stack([below[0], over[1]]))
    beside.append(jnp.stack([over[0], below[1]]))
    expected = jnp.stack(beside, axis=2)
    matches = a_cols.reshape(2, PLANE, 1, KC) == expected[..., None]
    chosen = jnp.sum(jnp.where(matches, jnp.arange(KC, dtype=jnp.int32), 0), axis=3)

    runs = p_cols[:PLANE].reshape(PY, PX)[:, 0] % RUNS
    down_in = (jnp.roll(runs, 1) == runs).astype(jnp.int32)
    up_in = (jnp.roll(runs, -1) == runs).astype(jnp.int32)

    def scalars(layer):
        owners = lax.dynamic_index_in_dim(
            coarse_owner, (position + layer) % layers, 0, keepdims=False
        )
        order = jnp.arange(AXY, dtype=jnp.int32)
        picked = jnp.sum(jnp.where(owners[None, :] == order[:, None], order[None, :], 0), axis=1)
        return jnp.concatenate([runs, down_in, up_in, picked])

    blocks = aligned(jnp.transpose(a_blocks, (1, 0, 2)), p_blocks, chosen.reshape(-1))
    upper = layer_part(blocks, 1, scalars(1), after, 5, 6, BF16)
    arrived = lax.ppermute(upper, axes, up)
    lower = layer_part(blocks, 0, scalars(0), before, 6, 5, F32)
    summed = (lower + arrived.astype(F32)).astype(BF16)
    placed = lax.all_to_all(summed, "slab", split_axis=0, concat_axis=0, tiled=True)
    return jnp.transpose(flattened(placed), (1, 0, 2))


def solution(mesh):
    return jax.shard_map(
        per_device,
        mesh=mesh,
        in_specs=(
            P(("slab", "grp"), None, None),
            P(("slab", "grp"), None),
            P(("slab", "grp"), None),
            P(("slab", "grp")),
            P(),
        ),
        out_specs=P(("slab", "grp"), None, None),
        check_vma=False,
    )
```

time: 185 us -> 149 us (0.81)
  waiting for transfers between devices: 36.4 us -> 1.37 us
  Pallas kernels: 56.5 us -> 79 us
  local copies, waits for them, and re-layouts: 32.7 us -> 11.9 us
  other arithmetic: 6.11 us -> 2.79 us
    ppermute x1, waiting for transfers between devices: 36.4 us -> 0.01 us  [per_device(): before = lax.ppermute(plane1, axes, up)]
    pallas_call x0 -> x2, Pallas kernels: none -> 29.6 us  [the longest x1 23.4 us: aligned(): pl.pallas_call(align_kernel, out_shape=(jax.ShapeDtypeStruct((KC, count,...]
    unnamed x9 -> x8, local copies, waits for them, and re-layouts: 18.4 us -> 4.02 us
    pallas_call x2, Pallas kernels: 56.5 us -> 49.4 us  [layer_part(): pl.pallas_call(functools.partial(layer_kernel, out_slot, zero_slot), out_...]
    convert_element_type x1, other arithmetic: 4 us -> 0.57 us  [per_device(): summed = (lower + arrived.astype(F32)).astype(BF16)]
    pallas_call x1 -> x0, local copies, waits for them, and re-layouts: 2.83 us -> none  [layer_part(): pl.pallas_call(functools.partial(layer_kernel, out_slot, zero_slot), out_...]
    all_to_all x1 -> x0, local copies, waits for them, and re-layouts: 2.37 us -> none  [per_device(): lax.all_to_all(summed, 'slab', split_axis=0, concat_axis=0, tiled=True)]
  transfers between devices with their start and end apart: 3 -> 3, of which waited for: 1 -> 1; matrix products, arithmetic and copies ran while one was open for 14% -> 5% of each run, Pallas kernels for 16% -> 33%
where the time goes in v2:
time: 149 us; the launch traced here: 148 us
  Pallas kernels  79 us (53%)
  blocking collectives  45.7 us (31%)
  local copies, waits for them, and re-layouts  11.9 us (8%)
  starting transfers between devices  6.43 us (4%)
  other arithmetic  2.79 us (2%)
    pallas_call x2, Pallas kernels, layer_part(): pl.pallas_call(functools.partial(layer_kernel, out_slot, zero_slot), out_...  49.4 us
    all_to_all x1, blocking collectives, per_device(): lax.all_to_all(summed, 'slab', split_axis=0, concat_axis=0, tiled=True)  45.7 us
    pallas_call x1, Pallas kernels, aligned(): pl.pallas_call(align_kernel, out_shape=(jax.ShapeDtypeStruct((KC, count,...  23.4 us
    pallas_call x1, Pallas kernels, flattened(): pl.pallas_call(flat_kernel, out_shape=jax.ShapeDtypeStruct((KC, rows, fla...  6.26 us
    ppermute x1, starting transfers between devices, per_device(): after = lax.ppermute(plane0, axes, down)  5.92 us
    unnamed x8, local copies, waits for them, and re-layouts  4.02 us
    slice x1, local copies, waits for them, and re-layouts, per_device(): plane1 = p_blocks[PLANE:]  3.25 us
  transfers between devices with their start and end apart: 3, of which 1 were waited for; matrix products, arithmetic and copies ran while one was open for 5% of the time, Pallas kernels for 33%

profile of v2, /device:TPU:0, one launch (start us, length us, event | category | flops | bytes accessed | tf_op | source)
XLA Modules:
  0.0 147.6 jit_solution(2361217052582878333)
XLA Ops:
  0.0 3.2 %fusion.11 = (bf16[128,4096]{1,0:T(8,128)(2,1)}, bf16[128,4096]{1,0:T(8,128)(2,1)}) fusion(bf16[256,4096]{1,0:T(8,128)(2,1)} %p_ref.1), kind=kLoop, calls=%fused_computation.81 | loop fusion | bytes 4194304 | tf_op jit(solution)/shard_map/slice | solution.py:270
  3.3 0.5 collective-permute-start.1
  3.7 5.9 %collective-permute-start = (bf16[128,4096]{1,0:T(8,128)(2,1)}, bf16[128,4096]{1,0:T(8,128)(2,1)}, u32[]{:S(2)}, u32[]{:S(2)}) collective-permute-start(bf16[128,4096]{1,0:T(8,128)(2,1)} %get-tuple-element.20), channel_id=1, source_target_pairs={{1,0},{2,1},{3,2},{4,3},{5,4},{6,5},{7,6},{8,7},{9,8},{10,9},{11,1... | collective-permute-start | bytes 3145736 | tf_op jit(solution)/shard_map/ppermute | solution.py:271
  9.9 0.1 and.153
  10.0 0.1 and.149
  10.2 0.1 and.151
  10.3 0.1 and.147
  10.4 0.1 and.145
  10.6 0.1 and.143
  10.8 0.1 iota.268
  10.9 0.1 iota.250
  11.0 0.1 iota.247
  11.1 0.1 iota.256
  11.2 0.1 reshape.891
  11.3 0.1 slice_reduce_fusion
  11.5 0.1 iota.265
  11.7 0.1 iota.259
  11.8 0.1 iota.241
  11.9 0.1 iota.232
  12.0 0.1 iota.229
  12.1 0.1 iota.223
  12.3 0.1 iota.220
  12.4 0.1 iota.238
  12.5 0.1 select_add_fusion.1
  12.6 0.1 slice.73
  12.7 0.1 slice.67
  12.8 0.1 slice.71
  12.9 0.1 slice.69
  13.1 0.1 constant_dynamic-update-slice_fusion.3
  13.1 0.1 constant_dynamic-update-slice_fusion.2
  13.3 0.1 copy.10
  13.5 0.2 reshape.892.scal
  13.7 23.4 %align_blocks.1 = (bf16[7,256,32,128]{3,2,1,0:T(8,128)(2,1)}, bf16[256,64,128]{2,1,0:T(8,128)(2,1)S(1)}, bf16[128,2,2,32,128]{4,3,2,1,0:T(8,128)(2,1)S(1)}) custom-call(s32[1792]{0:T(1024)S(1)} %reshape.892.scal, bf16[7,256,4096]{2,1,0:T(8,128)(2,1)} %bitcast.16, bf16[256,4096]{1,0:T(8,128)(2,1)S(1)} %copy-done.2), custom_call_target="tpu_custom_call" | custom-call | bytes 36700160 | tf_op jit(solution)/shard_map/align_blocks/pallas_call | solution.py:57
  37.1 2.0 %copy-done = bf16[256,64,128]{2,1,0:T(8,128)(2,1)} copy-done((bf16[256,64,128]{2,1,0:T(8,128)(2,1)}, bf16[256,64,128]{2,1,0:T(8,128)(2,1)S(1)}, u32[]{:S(2)}) %copy-start) | copy-done | bytes 4194328
  39.1 2.0 %copy-done.1 = bf16[128,2,2,32,128]{4,3,2,1,0:T(8,128)(2,1)} copy-done((bf16[128,2,2,32,128]{4,3,2,1,0:T(8,128)(2,1)}, bf16[128,2,2,32,128]{4,3,2,1,0:T(8,128)(2,1)S(1)}, u32[]{:S(2)}) %copy-start.1) | copy-done | bytes 4194328
  41.1 0.8 dynamic-slice_bitcast_fusion.1
  41.9 0.6 fusion.14
  42.5 0.1 select_reduce_fusion
  42.7 1.3 compare_convert_fusion.1
  44.0 0.1 pad_add_fusion.2
  44.0 24.7 %layer_upper.1 = bf16[32,7,32,128]{3,2,1,0:T(8,128)(2,1)S(1)} custom-call(s32[80]{0:T(128)S(1)} %get-tuple-element.15.scal, bf16[7,256,32,128]{3,2,1,0:T(8,128)(2,1)} %get-tuple-element.10.a_plane.a_down.a_up.a_zin.a_zout, bf16[7,256,32,128]{3,2,1,0:T(8,128)(2,1)} %get-tuple-element.10.a_plane.a_down.a_up.a_zin.a_zout, ...), custom_call_target="tpu_custom_call" | custom-call | flops 939524096 | bytes 7340032 | tf_op jit(solution)/shard_map/layer_upper/pallas_call | solution.py:205
  68.8 0.1 select_reduce_fusion.1
  68.9 0.1 pad_add_fusion.scal
  69.0 24.7 %layer_lower.1 = f32[32,7,32,128]{3,2,1,0:T(8,128)S(1)} custom-call(s32[80]{0:T(128)S(1)} %pad_add_fusion.scal, bf16[7,256,32,128]{3,2,1,0:T(8,128)(2,1)} %get-tuple-element.10.a_plane.a_down.a_up.a_zin.a_zout, bf16[7,256,32,128]{3,2,1,0:T(8,128)(2,1)} %get-tuple-element.10.a_plane.a_down.a_up.a_zin.a_zout, ...), custom_call_target="tpu_custom_call" | custom-call | flops 939524096 | bytes 7340032 | tf_op jit(solution)/shard_map/layer_lower/pallas_call | solution.py:205
  93.7 1.4 collective-permute-done.2
  95.1 0.6 add_convert_fusion
  95.6 45.7 %all_to_all.5.in_ref = bf16[32,7,32,128]{3,2,1,0:T(8,128)(2,1)} all-to-all(bf16[32,7,32,128]{3,2,1,0:T(8,128)(2,1)S(1)} %add_convert_fusion), channel_id=1, replica_groups=mesh['slab'=8,'grp'=4] {'slab'}, dimensions={0} | all-to-all | bytes 3670016 | tf_op jit(solution)/shard_map/all_to_all | solution.py:313
  141.3 6.3 %flatten_rows.1 = bf16[7,32,4096]{2,1,0:T(8,128)(2,1)} custom-call(bf16[32,7,32,128]{3,2,1,0:T(8,128)(2,1)} %all_to_all.5.in_ref), custom_call_target="tpu_custom_call" | custom-call | tf_op jit(solution)/shard_map/flatten_rows/pallas_call | solution.py:251
  (55 shorter events, 1.1 us)
Async XLA Ops:
  0.0 13.7 %copy-start.2 = (bf16[256,4096]{1,0:T(8,128)(2,1)S(1)}, bf16[256,4096]{1,0:T(8,128)(2,1)}, u32[]{:S(2)}) copy-start(bf16[256,4096]{1,0:T(8,128)(2,1)} %p_ref.1) | copy-start | bytes 6291460
  0.0 11.2 %slice-start = ((s32[256]{0:T(256)}), s32[128]{0:T(128)S(1)}, s32[]{:S(2)}) async-start(s32[256]{0:T(256)} %param.8), calls=%async_computation.1 | async-start | bytes 1024 | tf_op jit(solution)/shard_map/slice | solution.py:296
  0.0 13.3 %copy-start.3 = (s32[256,7]{0,1:T(8,128)S(1)}, s32[256,7]{0,1:T(8,128)}, u32[]{:S(2)}) copy-start(s32[256,7]{0,1:T(8,128)} %param.6) | copy-start | bytes 21508
  3.3 40.8 %collective-permute-start.1 = (bf16[128,4096]{1,0:T(8,128)(2,1)}, bf16[128,4096]{1,0:T(8,128)(2,1)S(1)}, u32[]{:S(2)}, u32[]{:S(2)}) collective-permute-start(bf16[128,4096]{1,0:T(8,128)(2,1)} %get-tuple-element.19), channel_id=1, source_target_pairs={{0,1},{1,2},{2,3},{3,4},{4,5},{5,6},{6,7},{7,8},{8,9},{9,10},{10,1... | collective-permute-start | bytes 3145736 | tf_op jit(solution)/shard_map/ppermute | solution.py:272
  3.7 40.3 %collective-permute-start = (bf16[128,4096]{1,0:T(8,128)(2,1)}, bf16[128,4096]{1,0:T(8,128)(2,1)}, u32[]{:S(2)}, u32[]{:S(2)}) collective-permute-start(bf16[128,4096]{1,0:T(8,128)(2,1)} %get-tuple-element.20), channel_id=1, source_target_pairs={{1,0},{2,1},{3,2},{4,3},{5,4},{6,5},{7,6},{8,7},{9,8},{10,9},{11,1... | collective-permute-start | bytes 3145736 | tf_op jit(solution)/shard_map/ppermute | solution.py:271
  37.1 2.0 %copy-start = (bf16[256,64,128]{2,1,0:T(8,128)(2,1)}, bf16[256,64,128]{2,1,0:T(8,128)(2,1)S(1)}, u32[]{:S(2)}) copy-start(bf16[256,64,128]{2,1,0:T(8,128)(2,1)S(1)} %get-tuple-element.11.p_own.p_out) | copy-start | bytes 12582916
  39.1 2.0 %copy-start.1 = (bf16[128,2,2,32,128]{4,3,2,1,0:T(8,128)(2,1)}, bf16[128,2,2,32,128]{4,3,2,1,0:T(8,128)(2,1)S(1)}, u32[]{:S(2)}) copy-start(bf16[128,2,2,32,128]{4,3,2,1,0:T(8,128)(2,1)S(1)} %get-tuple-element.13.plhs) | copy-start | bytes 12582916
  68.8 26.3 %collective-permute-start.2 = (bf16[32,7,32,128]{3,2,1,0:T(8,128)(2,1)S(1)}, bf16[32,7,32,128]{3,2,1,0:T(8,128)(2,1)S(1)}, u32[]{:S(2)}, u32[]{:S(2)}) collective-permute-start(bf16[32,7,32,128]{3,2,1,0:T(8,128)(2,1)S(1)} %layer_upper.1), channel_id=1, source_target_pairs={{0,1},{1,2},{2,3},{3,4},{4,5},{5,6},{6,7},{7,8},{8,9},{9,10},{10,1... | collective-permute-start | bytes 5505032 | tf_op jit(solution)/shard_map/ppermute | solution.py:310

commit v3 on v2

v3 whole, which is shorter than its diff:
```python
import functools

import jax
import jax.numpy as jnp
from jax import lax
from jax.experimental import pallas as pl
from jax.experimental.pallas import tpu as pltpu
from jax.sharding import PartitionSpec as P

KC = 7
PX = 8
PY = 16
RUNS = 8
AXY = 32
PLANE = PX * PY
BS = 64
HALF = BS // 2
WIDE = 2 * BS
F32 = jnp.float32
BF16 = jnp.bfloat16
NEAR = 5
PITCH = 17


def swap(x):
    return pltpu.roll(x, BS, 1)


def spread(val, low, store):
    turned = swap(val)
    store[pl.ds(0, HALF, stride=2), :] = jnp.where(low, val, turned)
    store[pl.ds(1, HALF, stride=2), :] = jnp.where(low, turned, val)
    return turned


def align_kernel(scal, a_ref, p_ref, near, far, prel, plhs, tmp, vtmp):
    step = pl.program_id(0)
    rows = a_ref.shape[1]
    low = lax.broadcasted_iota(jnp.int32, (HALF, WIDE), 1) < BS
    for k in range(KC):
        for i in range(HALF):
            tmp[k, i * PITCH : i * PITCH + rows, :] = a_ref[k, :, i * WIDE : (i + 1) * WIDE].astype(F32)
    for i in range(HALF):
        tmp[KC, i * PITCH : i * PITCH + rows, :] = p_ref[:, i * WIDE : (i + 1) * WIDE].astype(F32)
    for r in range(rows):
        for j in range(KC):
            k = scal[(step * rows + r) * KC + j]
            block = tmp[k, pl.ds(r, HALF, stride=PITCH), :].astype(BF16)
            if j < NEAR:
                near[j, r] = block
            else:
                far[j - NEAR, r] = block
        val = tmp[KC, pl.ds(r, HALF, stride=PITCH), :]
        turned = spread(val, low, vtmp.at[r])
        prel[r] = vtmp[r].astype(BF16)
        plhs[r // 2, r % 2, 0] = val.astype(BF16)
        plhs[r // 2, r % 2, 1] = turned.astype(BF16)


def aligned(a_blocks, p_blocks, chosen):
    rows = 16
    count, flat = p_blocks.shape
    return pl.pallas_call(
        align_kernel,
        out_shape=(
            jax.ShapeDtypeStruct((NEAR, count, HALF, WIDE), BF16),
            jax.ShapeDtypeStruct((KC - NEAR, count, HALF, WIDE), BF16),
            jax.ShapeDtypeStruct((count, BS, WIDE), BF16),
            jax.ShapeDtypeStruct((count // 2, 2, 2, HALF, WIDE), BF16),
        ),
        grid_spec=pltpu.PrefetchScalarGridSpec(
            num_scalar_prefetch=1,
            grid=(count // rows,),
            in_specs=[
                pl.BlockSpec((KC, rows, flat), lambda s, _: (0, s, 0)),
                pl.BlockSpec((rows, flat), lambda s, _: (s, 0)),
            ],
            out_specs=(
                pl.BlockSpec((NEAR, rows, HALF, WIDE), lambda s, _: (0, s, 0, 0)),
                pl.BlockSpec((KC - NEAR, rows, HALF, WIDE), lambda s, _: (0, s, 0, 0)),
                pl.BlockSpec((rows, BS, WIDE), lambda s, _: (s, 0, 0)),
                pl.BlockSpec((rows // 2, 2, 2, HALF, WIDE), lambda s, _: (s, 0, 0, 0, 0)),
            ),
            scratch_shapes=[
                pltpu.VMEM((KC + 1, PITCH * HALF, WIDE), F32),
                pltpu.VMEM((rows, BS, WIDE), F32),
            ],
        ),
        compiler_params=pltpu.CompilerParams(vmem_limit_bytes=32 * 1024 * 1024),
        cost_estimate=pl.CostEstimate(
            flops=0, bytes_accessed=5 * KC * count * flat, transcendentals=0
        ),
        name="align_blocks",
    )(chosen, a_blocks, p_blocks)


def lane_masks():
    low = lax.broadcasted_iota(jnp.int32, (HALF, WIDE), 1) < BS
    low2 = lax.broadcasted_iota(jnp.int32, (BS, WIDE), 1) < BS
    return low, low2


def both(block, low2):
    dup = block.astype(F32)
    top = jnp.where(low2, dup, 0.0)
    bottom = jnp.where(low2, 0.0, dup)
    return jnp.concatenate([top, bottom], axis=0).astype(BF16)


def pair(a, b, low):
    return jnp.concatenate(
        [jnp.where(low, a, swap(b)), jnp.where(low, swap(a), b)], axis=0
    ).astype(BF16)


def add_product(acc, plhs, at, q, parts):
    lhs = plhs[at].reshape(2 * BS, WIDE)[:, :BS]
    for b, part in enumerate(parts):
        acc[q, b] += lax.dot_general(
            lhs,
            jnp.concatenate(part, axis=0),
            (((0,), (0,)), ((), ())),
            preferred_element_type=F32,
        )


def write_rows(scal, acc, out_ref, low):
    def write_row(o, _):
        q = scal[3 * PY + o]
        for b in range(2):
            even = acc[q, b, pl.ds(0, HALF, stride=2), :]
            odd = acc[q, b, pl.ds(1, HALF, stride=2), :]
            out_ref[o, 2 * b] = jnp.where(low, even, swap(odd)).astype(out_ref.dtype)
            if b == 0:
                out_ref[o, 1] = jnp.where(low, swap(even), odd).astype(out_ref.dtype)
        return 0

    lax.fori_loop(0, AXY, write_row, 0)


def outer_x(x):
    return (x - 1) % PX if x % 2 == 0 else (x + 1) % PX


def far_kernel(scal, blocks, p_own, p_out, plhs, out_ref, carried, acc):
    low, low2 = lane_masks()

    def carry_row(y, _):
        for x in range(PX):
            g = y * PX + x
            f = y * PX + outer_x(x)
            carried[0, f] = jnp.dot(blocks[0, f], both(p_own[g], low2), preferred_element_type=F32)
            carried[1, g] = jnp.dot(blocks[1, g], both(p_out[g], low2), preferred_element_type=F32)
        return 0

    lax.fori_loop(0, PY, carry_row, 0)
    acc[...] = jnp.zeros_like(acc)

    def sum_row(y, _):
        run = scal[y]
        zero = jnp.zeros((HALF, WIDE), F32)
        for c in range(PX // 2):
            parts = ([], [])
            for e in range(2):
                f = y * PX + 2 * c + e
                side = carried[0, f]
                parts[0].append(pair(side, zero, low) if e == 0 else pair(zero, side, low))
                parts[1].append(pair(carried[1, f], zero, low))
            add_product(acc, plhs, (y * PX) // 2 + c, c * RUNS + run, parts)
        return 0

    lax.fori_loop(0, PY, sum_row, 0)
    write_rows(scal, acc, out_ref, low)


def near_kernel(scal, blocks, p_own, zin_ref, plhs, out_ref, ptmp, vtmp, pin, carried, acc):
    low, low2 = lane_masks()
    rows = 16

    def some(n, _):
        part = zin_ref[pl.ds(pl.multiple_of(n * rows, rows), rows), :]
        for i in range(HALF):
            ptmp[i * PITCH : i * PITCH + rows, :] = part[:, i * WIDE : (i + 1) * WIDE].astype(F32)
        for r in range(rows):
            spread(ptmp[pl.ds(r, HALF, stride=PITCH), :], low, vtmp.at[r])
            pin[n * rows + r] = vtmp[r].astype(BF16)
        return 0

    lax.fori_loop(0, PLANE // rows, some, 0)

    def carry_row(y, _):
        above = lax.rem(y + 1, PY)
        below = lax.rem(y + PY - 1, PY)
        for x in range(PX):
            g = y * PX + x
            takers = (g, y * PX + (x ^ 1), above * PX + x, below * PX + x)
            lhs = jnp.concatenate([blocks[j, f] for j, f in enumerate(takers)], axis=0)
            got = jnp.dot(lhs, both(p_own[g], low2), preferred_element_type=F32).astype(BF16)
            for j, f in enumerate(takers):
                carried[j, f] = got[j * HALF : (j + 1) * HALF]
            carried[4, g] = jnp.dot(
                blocks[4, g], both(pin[g], low2), preferred_element_type=F32
            ).astype(BF16)
        return 0

    lax.fori_loop(0, PY, carry_row, 0)
    acc[...] = jnp.zeros_like(acc)

    def sum_row(y, _):
        run = scal[y]
        down_in = scal[PY + y] != 0
        up_in = scal[2 * PY + y] != 0
        zero = jnp.zeros((HALF, WIDE), F32)
        for c in range(PX // 2):
            parts = ([], [])
            for e in range(2):
                f = y * PX + 2 * c + e
                own, inner, down, up, zin = (carried[j, f].astype(F32) for j in range(NEAR))
                kept = (own + inner) + zin
                kept = kept + jnp.where(down_in, down, zero) + jnp.where(up_in, up, zero)
                down = jnp.where(down_in, zero, down)
                up = jnp.where(up_in, zero, up)
                parts[0].append(pair(down, up, low))
                parts[1].append(pair(kept, zero, low))
            add_product(acc, plhs, (y * PX) // 2 + c, c * RUNS + run, parts)
        return 0

    lax.fori_loop(0, PY, sum_row, 0)
    write_rows(scal, acc, out_ref, low)


def layer_part(kernel, name, layer, dtype, scalars, blocks, prel, plhs, zin=None):
    count = blocks.shape[0]
    flat = BS * BS
    plane = pl.BlockSpec((PLANE, BS, WIDE), lambda s, _: (layer, 0, 0))
    if zin is None:
        last = (pl.BlockSpec((PLANE, BS, WIDE), lambda s, _: (1 - layer, 0, 0)), prel)
        scratch = [pltpu.VMEM((KC - NEAR, PLANE, HALF, WIDE), F32)]
    else:
        last = (pl.BlockSpec((PLANE, flat), lambda s, _: (0, 0)), zin)
        scratch = [
            pltpu.VMEM((PITCH * HALF, WIDE), F32),
            pltpu.VMEM((16, BS, WIDE), F32),
            pltpu.VMEM((PLANE, BS, WIDE), BF16),
            pltpu.VMEM((NEAR, PLANE, HALF, WIDE), BF16),
        ]
    return pl.pallas_call(
        kernel,
        out_shape=jax.ShapeDtypeStruct((AXY, 3, HALF, WIDE), dtype),
        grid_spec=pltpu.PrefetchScalarGridSpec(
            num_scalar_prefetch=1,
            grid=(1,),
            in_specs=[
                pl.BlockSpec((count, PLANE, HALF, WIDE), lambda s, _: (0, layer, 0, 0)),
                plane,
                last[0],
                pl.BlockSpec((PLANE // 2, 2, 2, HALF, WIDE), lambda s, _: (layer, 0, 0, 0, 0)),
            ],
            out_specs=pl.BlockSpec((AXY, 3, HALF, WIDE), lambda s, _: (0, 0, 0, 0)),
            scratch_shapes=scratch + [pltpu.VMEM((AXY, 2, BS, WIDE), F32)],
        ),
        compiler_params=pltpu.CompilerParams(vmem_limit_bytes=44 * 1024 * 1024),
        cost_estimate=pl.CostEstimate(
            flops=PLANE * count * 64 * BS**3,
            bytes_accessed=PLANE * count * flat * 2,
            transcendentals=0,
        ),
        name=name + ("_upper" if layer else "_lower"),
    )(scalars, blocks, prel, last[1], plhs)


def flat_kernel(in_ref, *refs):
    out_ref, tmp = refs[-2:]
    rows = in_ref.shape[0]
    for o in range(rows):
        tmp[o * (HALF + 1) : o * (HALF + 1) + HALF] = in_ref[o, 0].astype(F32)
    for i in range(HALF):
        out_ref[0, :, i * WIDE : (i + 1) * WIDE] = tmp[pl.ds(i, rows, stride=HALF + 1), :].astype(BF16)


def flattened(blocks, slot_of_part, into=None):
    rows, parts = blocks.shape[:2]
    flat = BS * BS
    kept = [] if into is None else [into]
    return pl.pallas_call(
        flat_kernel,
        out_shape=jax.ShapeDtypeStruct((KC, rows, flat), BF16),
        grid=(parts,),
        in_specs=[pl.BlockSpec((rows, 1, HALF, WIDE), lambda s: (0, s, 0, 0))]
        + [pl.BlockSpec(memory_space=pl.ANY) for _ in kept],
        out_specs=pl.BlockSpec((1, rows, flat), lambda s: (slot_of_part(s), 0, 0)),
        scratch_shapes=[pltpu.VMEM((rows * (HALF + 1), WIDE), F32)],
        input_output_aliases={1: 0} if kept else {},
        name="flatten_" + ("near" if kept else "far"),
    )(blocks, *kept)


def per_device(a_blocks, a_cols, p_blocks, p_cols, coarse_owner):
    axes = ("slab", "grp")
    layers = lax.axis_size(axes)
    position = lax.axis_index(axes)
    depth_total = 2 * layers
    up = [(i, (i + 1) % layers) for i in range(layers)]
    down = [(j, i) for i, j in up]
    plane0 = p_blocks[:PLANE]
    plane1 = p_blocks[PLANE:]
    after = lax.ppermute(plane0, axes, down)
    before = lax.ppermute(plane1, axes, up)
    after, before = lax.optimization_barrier((after, before))

    depth = 2 * position + lax.broadcasted_iota(jnp.int32, (2, PY, PX), 0)
    ypos = lax.broadcasted_iota(jnp.int32, (2, PY, PX), 1)
    xpos = lax.broadcasted_iota(jnp.int32, (2, PY, PX), 2)

    def locate(zz, yy, xx):
        return ((zz % depth_total * PY + yy % PY) * PX + xx % PX).reshape(2, PLANE)

    beside = [
        locate(depth, ypos, xpos),
        locate(depth, ypos, xpos + 1 - 2 * (xpos % 2)),
        locate(depth, ypos - 1, xpos),
        locate(depth, ypos + 1, xpos),
    ]
    below, over = locate(depth - 1, ypos, xpos), locate(depth + 1, ypos, xpos)
    beside.append(jnp.stack([below[0], over[1]]))
    beside.append(locate(depth, ypos, xpos - 1 + 2 * (xpos % 2)))
    beside.append(jnp.stack([over[0], below[1]]))
    expected = jnp.stack(beside, axis=2)
    matches = a_cols.reshape(2, PLANE, 1, KC) == expected[..., None]
    chosen = jnp.sum(jnp.where(matches, jnp.arange(KC, dtype=jnp.int32), 0), axis=3)

    runs = p_cols[:PLANE].reshape(PY, PX)[:, 0] % RUNS
    down_in = (jnp.roll(runs, 1) == runs).astype(jnp.int32)
    up_in = (jnp.roll(runs, -1) == runs).astype(jnp.int32)

    def scalars(layer):
        owners = lax.dynamic_index_in_dim(
            coarse_owner, (position + layer) % layers, 0, keepdims=False
        )
        order = jnp.arange(AXY, dtype=jnp.int32)
        picked = jnp.sum(jnp.where(owners[None, :] == order[:, None], order[None, :], 0), axis=1)
        return jnp.concatenate([runs, down_in, up_in, picked])

    near, far, prel, plhs = aligned(jnp.transpose(a_blocks, (1, 0, 2)), p_blocks, chosen.reshape(-1))
    scal = (scalars(0), scalars(1))

    def exchanged(rows):
        return lax.all_to_all(rows, "slab", split_axis=0, concat_axis=0, tiled=True)

    upper = layer_part(far_kernel, "far", 1, BF16, scal[1], far, prel, plhs)
    arrived = lax.ppermute(upper, axes, up)
    lower = layer_part(far_kernel, "far", 0, F32, scal[0], far, prel, plhs)
    sides = (lower[:, :2] + arrived[:, :2].astype(F32)).astype(BF16)
    far_rows = jnp.concatenate([sides, arrived[:, 2:], lower[:, 2:].astype(BF16)], axis=1)
    far_rows, near = lax.optimization_barrier((far_rows, near))
    far_rows = exchanged(far_rows)

    upper = layer_part(near_kernel, "near", 1, BF16, scal[1], near, prel, plhs, after)
    arrived = lax.ppermute(upper, axes, up)
    lower = layer_part(near_kernel, "near", 0, F32, scal[0], near, prel, plhs, before)
    near_rows = exchanged((lower + arrived.astype(F32)).astype(BF16))

    flat = flattened(far_rows, lambda s: jnp.where(s < 2, s + 1, s + 3))
    flat = flattened(near_rows, lambda s: jnp.where(s < 2, s + 3, 0), flat)
    return jnp.transpose(flat, (1, 0, 2))


def solution(mesh):
    return jax.shard_map(
        per_device,
        mesh=mesh,
        in_specs=(
            P(("slab", "grp"), None, None),
            P(("slab", "grp"), None),
            P(("slab", "grp"), None),
            P(("slab", "grp")),
            P(),
        ),
        out_specs=P(("slab", "grp"), None, None),
        check_vma=False,
    )
```

time: 149 us -> 149 us (level)
  blocking collectives: 45.7 us -> 0 us
  starting transfers between devices: 6.43 us -> 24.8 us
  waiting for transfers between devices: 1.37 us -> 17.8 us
  Pallas kernels: 79 us -> 84.1 us
  local copies, waits for them, and re-layouts: 11.9 us -> 16.5 us
  other arithmetic: 2.79 us -> 4.77 us
    all_to_all x1 -> x0, blocking collectives: 45.7 us -> none  [per_device(): lax.all_to_all(summed, 'slab', split_axis=0, concat_axis=0, tiled=True)]
    all_to_all x0 -> x2, waiting for transfers between devices: none -> 17.4 us  [exchanged(): return lax.all_to_all(rows, 'slab', split_axis=0, concat_axis=0, tiled=True)]
    ppermute x1 -> x2, starting transfers between devices: 0.06 us -> 11.8 us  [per_device(): arrived = lax.ppermute(upper, axes, up)]
    all_to_all x0 -> x2, starting transfers between devices: none -> 7.14 us  [exchanged(): return lax.all_to_all(rows, 'slab', split_axis=0, concat_axis=0, tiled=True)]
    unnamed x8 -> x16, local copies, waits for them, and re-layouts: 4.02 us -> 8.92 us
    pallas_call x3 -> x5, Pallas kernels: 72.8 us -> 77.6 us  [the longest x4 60.5 us: layer_part(): pl.pallas_call(kernel, out_shape=jax.ShapeDtypeStruct((AXY, 3, HALF, WIDE...]
    slice x1, local copies, waits for them, and re-layouts: 3.25 us -> 1.54 us  [per_device(): plane1 = p_blocks[PLANE:]]
    pallas_call x1 -> x2, Pallas kernels: 6.26 us -> 6.49 us  [flattened(): pl.pallas_call(flat_kernel, out_shape=jax.ShapeDtypeStruct((KC, rows, fla...]
  transfers between devices with their start and end apart: 3 -> 6, of which waited for: 1 -> 2; matrix products, arithmetic and copies ran while one was open for 5% -> 3% of each run, Pallas kernels for 33% -> 34%
where the time goes in v3:
time: 149 us; the launch traced here: 148 us
  Pallas kernels  84.1 us (56%)
  starting transfers between devices  24.8 us (17%)
  waiting for transfers between devices  17.8 us (12%)
  local copies, waits for them, and re-layouts  16.5 us (11%)
  other arithmetic  4.77 us (3%)
    pallas_call x4, Pallas kernels, layer_part(): pl.pallas_call(kernel, out_shape=jax.ShapeDtypeStruct((AXY, 3, HALF, WIDE...  60.5 us
    all_to_all x2, waiting for transfers between devices, exchanged(): return lax.all_to_all(rows, 'slab', split_axis=0, concat_axis=0, tiled=True)  17.4 us
    pallas_call x1, Pallas kernels, aligned(): pl.pallas_call(align_kernel, out_shape=(jax.ShapeDtypeStruct((NEAR, count...  17.1 us
    ppermute x2, starting transfers between devices, per_device(): arrived = lax.ppermute(upper, axes, up)  11.8 us
    unnamed x16, local copies, waits for them, and re-layouts  8.92 us
    all_to_all x2, starting transfers between devices, exchanged(): return lax.all_to_all(rows, 'slab', split_axis=0, concat_axis=0, tiled=True)  7.14 us
    pallas_call x2, Pallas kernels, flattened(): pl.pallas_call(flat_kernel, out_shape=jax.ShapeDtypeStruct((KC, rows, fla...  6.49 us
    ppermute x1, starting transfers between devices, per_device(): after = lax.ppermute(plane0, axes, down)  5.88 us
  transfers between devices with their start and end apart: 6, of which 2 were waited for; matrix products, arithmetic and copies ran while one was open for 3% of the time, Pallas kernels for 34%

profile of v3, /device:TPU:0, one launch (start us, length us, event | category | flops | bytes accessed | tf_op | source)
XLA Modules:
  0.0 148.3 jit_solution(10954659452984151069)
XLA Ops:
  0.2 0.7 slice.73
  1.0 0.1 slice_reduce_fusion
  1.1 0.6 fusion.17
  1.8 0.1 iota.241
  2.0 0.1 and.176
  2.2 0.1 iota.232
  2.3 0.1 iota.235
  2.5 0.1 and.174
  2.6 0.1 and.178
  3.1 0.1 iota.265
  3.2 0.1 and.181
  3.4 0.1 iota.262
  3.6 0.1 iota.271
  3.7 0.1 iota.274
  3.9 0.1 and.183
  4.0 0.1 select_add_fusion.1
  4.4 0.1 slice.84
  4.5 0.1 slice.86
  4.6 0.7 eq.86
  5.6 0.1 copy.11
  5.8 0.2 reshape.1007.scal
  6.0 0.8 dynamic-slice_bitcast_fusion.1
  6.8 0.1 select_reduce_fusion
  6.9 1.6 %copy-done.4 = bf16[256,4096]{1,0:T(8,128)(2,1)S(1)} copy-done((bf16[256,4096]{1,0:T(8,128)(2,1)S(1)}, bf16[256,4096]{1,0:T(8,128)(2,1)}, u32[]{:S(2)}) %copy-start.4) | copy-done | bytes 2097176
  8.5 17.1 %align_blocks.1 = (bf16[5,256,32,128]{3,2,1,0:T(8,128)(2,1)}, bf16[2,256,32,128]{3,2,1,0:T(8,128)(2,1)S(1)}, bf16[256,64,128]{2,1,0:T(8,128)(2,1)S(1)}, bf16[128,2,2,32,128]{4,3,2,1,0:T(8,128)(2,1)S(1)}) custom-call(s32[1792]{0:T(1024)S(1)} %reshape.1007.scal, bf16[7,256,4096]{2,1,0:T(8,128)(2,1)} %bitcast.16, bf16[256,4096]{1,0:T(8,128)(2,1)S(1)} %copy-done.4), custom_call_target="tpu_custom_call" | custom-call | bytes 36700160 | tf_op jit(solution)/shard_map/align_blocks/pallas_call | solution.py:63
  25.6 2.1 %copy-done.2 = bf16[128,2,2,32,128]{4,3,2,1,0:T(8,128)(2,1)} copy-done((bf16[128,2,2,32,128]{4,3,2,1,0:T(8,128)(2,1)}, bf16[128,2,2,32,128]{4,3,2,1,0:T(8,128)(2,1)S(1)}, u32[]{:S(2)}) %copy-start.2) | copy-done | bytes 4194328
  27.6 1.3 compare_convert_fusion.1
  29.1 13.7 %far_upper.1 = bf16[32,3,32,128]{3,2,1,0:T(8,128)(2,1)S(1)} custom-call(s32[80]{0:T(128)S(1)} %get-tuple-element.21.scal, bf16[2,256,32,128]{3,2,1,0:T(8,128)(2,1)S(1)} %get-tuple-element.13.blocks, bf16[256,64,128]{2,1,0:T(8,128)(2,1)S(1)} %get-tuple-element.14.p_own.p_out, bf16[256,64,128]{2,1,0:T(8,128)(2,1)S(1)} %get-tuple-element.14.p_own.p_out, ...), custom_call_target="tpu_custom_call" | custom-call | flops 4294967296 | bytes 2097152 | tf_op jit(solution)/shard_map/far_upper/pallas_call | solution.py:247
  42.8 0.5 collective-permute-start
  43.3 1.5 %fusion.14 = (bf16[128,4096]{1,0:T(8,128)(2,1)}, bf16[128,4096]{1,0:T(8,128)(2,1)}) fusion(bf16[256,4096]{1,0:T(8,128)(2,1)S(1)} %copy-done.5), kind=kLoop, calls=%fused_computation.91 | loop fusion | bytes 4194304 | tf_op jit(solution)/shard_map/slice | solution.py:306
  44.8 5.9 %collective-permute-start.1 = (bf16[128,4096]{1,0:T(8,128)(2,1)}, bf16[128,4096]{1,0:T(8,128)(2,1)S(1)}, u32[]{:S(2)}, u32[]{:S(2)}) collective-permute-start(bf16[128,4096]{1,0:T(8,128)(2,1)} %get-tuple-element.26), channel_id=1, source_target_pairs={{1,0},{2,1},{3,2},{4,3},{5,4},{6,5},{7,6},{8,7},{9,8},{10,9},{11,1... | collective-permute-start | bytes 3145736 | tf_op jit(solution)/shard_map/ppermute | solution.py:307
  50.7 0.1 select_reduce_fusion.1
  50.9 13.9 %far_lower.1 = f32[32,3,32,128]{3,2,1,0:T(8,128)S(1)} custom-call(s32[80]{0:T(128)S(1)} %pad_add_fusion.scal, bf16[2,256,32,128]{3,2,1,0:T(8,128)(2,1)S(1)} %get-tuple-element.13.blocks, bf16[256,64,128]{2,1,0:T(8,128)(2,1)S(1)} %get-tuple-element.14.p_own.p_out, bf16[256,64,128]{2,1,0:T(8,128)(2,1)S(1)} %get-tuple-element.14.p_own.p_out, ...), custom_call_target="tpu_custom_call" | custom-call | flops 4294967296 | bytes 2097152 | tf_op jit(solution)/shard_map/far_lower/pallas_call | solution.py:247
  64.9 0.2 fusion
  65.1 1.1 pad_maximum_fusion
  66.2 3.6 %all-to-all-start.1 = ((bf16[32,4,32,128]{3,2,1,0:T(8,128)(2,1)}), bf16[32,4,32,128]{3,2,1,0:T(8,128)(2,1)S(1)}, u32[]{:S(2)}, u32[]{:S(2)}) async-start(bf16[32,4,32,128]{3,2,1,0:T(8,128)(2,1)} %pad_maximum_fusion), calls=%async_computation.1 | async-start | bytes 2097152 | tf_op jit(solution)/shard_map/all_to_all | solution.py:348
  69.8 0.4 collective-permute-done.2.zin_ref
  70.2 2.2 %copy-done.1 = bf16[256,64,128]{2,1,0:T(8,128)(2,1)S(1)} copy-done((bf16[256,64,128]{2,1,0:T(8,128)(2,1)S(1)}, bf16[256,64,128]{2,1,0:T(8,128)(2,1)}, u32[]{:S(2)}) %copy-start.1) | copy-done | bytes 4194328
  72.4 2.2 %copy-done.3 = bf16[128,2,2,32,128]{4,3,2,1,0:T(8,128)(2,1)S(1)} copy-done((bf16[128,2,2,32,128]{4,3,2,1,0:T(8,128)(2,1)S(1)}, bf16[128,2,2,32,128]{4,3,2,1,0:T(8,128)(2,1)}, u32[]{:S(2)}) %copy-start.3) | copy-done | bytes 4194328
  74.5 16.0 %near_upper.1 = bf16[32,3,32,128]{3,2,1,0:T(8,128)(2,1)S(1)} custom-call(s32[80]{0:T(128)S(1)} %get-tuple-element.21.scal, bf16[5,256,32,128]{3,2,1,0:T(8,128)(2,1)} %get-tuple-element.17.blocks, bf16[256,64,128]{2,1,0:T(8,128)(2,1)S(1)} %copy-done.1, bf16[128,4096]{1,0:T(8,128)(2,1)S(1)} %collective-permute-done.1.zin_ref, ...), custom_call_target="tpu_custom_call" | custom-call | flops 10737418240 | bytes 5242880 | tf_op jit(solution)/shard_map/near_upper/pallas_call | solution.py:247
  90.6 11.3 %collective-permute-start.3 = (bf16[32,3,32,128]{3,2,1,0:T(8,128)(2,1)S(1)}, bf16[32,3,32,128]{3,2,1,0:T(8,128)(2,1)S(1)}, u32[]{:S(2)}, u32[]{:S(2)}) collective-permute-start(bf16[32,3,32,128]{3,2,1,0:T(8,128)(2,1)S(1)} %near_upper.1), channel_id=1, source_target_pairs={{0,1},{1,2},{2,3},{3,4},{4,5},{5,6},{6,7},{7,8},{8,9},{9,10},{10,1... | collective-permute-start | bytes 2359304 | tf_op jit(solution)/shard_map/ppermute | solution.py:359
  101.9 16.8 %near_lower.1 = f32[32,3,32,128]{3,2,1,0:T(8,128)S(1)} custom-call(s32[80]{0:T(128)S(1)} %pad_add_fusion.scal, bf16[5,256,32,128]{3,2,1,0:T(8,128)(2,1)} %get-tuple-element.17.blocks, bf16[256,64,128]{2,1,0:T(8,128)(2,1)S(1)} %copy-done.1, bf16[128,4096]{1,0:T(8,128)(2,1)S(1)} %collective-permute-done.2.zin_ref, bf16[128,2,2,32,128]{4,3,2,1,0:T(8,128)(2,1)} %copy-done.2), custom_call_target="tpu_custom_call" | custom-call | flops 10737418240 | bytes 5242880 | tf_op jit(solution)/shard_map/near_lower/pallas_call | solution.py:247
  118.7 1.2 add_convert_fusion
  119.9 3.6 %all-to-all-start = ((bf16[32,3,32,128]{3,2,1,0:T(8,128)(2,1)}), bf16[32,3,32,128]{3,2,1,0:T(8,128)(2,1)S(1)}, u32[]{:S(2)}, u32[]{:S(2)}) async-start(bf16[32,3,32,128]{3,2,1,0:T(8,128)(2,1)} %add_convert_fusion), calls=%async_computation | async-start | bytes 1572864 | tf_op jit(solution)/shard_map/all_to_all | solution.py:348
  123.5 3.5 %flatten_far.1.refs_0_ = bf16[7,32,4096]{2,1,0:T(8,128)(2,1)} custom-call(bf16[32,4,32,128]{3,2,1,0:T(8,128)(2,1)} %copy-done.6), custom_call_target="tpu_custom_call" | custom-call | tf_op jit(solution)/shard_map/flatten_far/pallas_call | solution.py:285
  127.0 17.4 %all-to-all-done.in_ref = bf16[32,3,32,128]{3,2,1,0:T(8,128)(2,1)S(1)} async-done(((bf16[32,3,32,128]{3,2,1,0:T(8,128)(2,1)}), bf16[32,3,32,128]{3,2,1,0:T(8,128)(2,1)S(1)}, u32[]{:S(2)}, u32[]{:S(2)}) %all-to-all-start) | async-done | bytes 786464 | tf_op jit(solution)/shard_map/all_to_all | solution.py:348
  144.4 0.9 copy-done.7
  145.3 3.0 %flatten_near.1 = bf16[7,32,4096]{2,1,0:T(8,128)(2,1)} custom-call(bf16[32,3,32,128]{3,2,1,0:T(8,128)(2,1)} %copy-done.7, bf16[7,32,4096]{2,1,0:T(8,128)(2,1)} %flatten_far.1.refs_0_), custom_call_target="tpu_custom_call", output_to_operand_aliasing={{}: (1, {})} | custom-call | tf_op jit(solution)/shard_map/flatten_near/pallas_call | solution.py:285
  (73 shorter events, 2.1 us)
Async XLA Ops:
  6.9 1.6 %copy-start.4 = (bf16[256,4096]{1,0:T(8,128)(2,1)S(1)}, bf16[256,4096]{1,0:T(8,128)(2,1)}, u32[]{:S(2)}) copy-start(bf16[256,4096]{1,0:T(8,128)(2,1)} %p_ref.1) | copy-start | bytes 6291460
  25.6 2.1 %copy-start.2 = (bf16[128,2,2,32,128]{4,3,2,1,0:T(8,128)(2,1)}, bf16[128,2,2,32,128]{4,3,2,1,0:T(8,128)(2,1)S(1)}, u32[]{:S(2)}) copy-start(bf16[128,2,2,32,128]{4,3,2,1,0:T(8,128)(2,1)S(1)} %get-tuple-element.15.plhs) | copy-start | bytes 12582916
  27.6 23.3 %copy-start = (bf16[256,64,128]{2,1,0:T(8,128)(2,1)}, bf16[256,64,128]{2,1,0:T(8,128)(2,1)S(1)}, u32[]{:S(2)}) copy-start(bf16[256,64,128]{2,1,0:T(8,128)(2,1)S(1)} %get-tuple-element.14.p_own.p_out) | copy-start | bytes 12582916
  29.1 14.2 %copy-start.5 = (bf16[256,4096]{1,0:T(8,128)(2,1)S(1)}, bf16[256,4096]{1,0:T(8,128)(2,1)}, u32[]{:S(2)}) copy-start(bf16[256,4096]{1,0:T(8,128)(2,1)} %p_ref.1) | copy-start | bytes 6291460
  42.8 22.0 %collective-permute-start = (bf16[32,3,32,128]{3,2,1,0:T(8,128)(2,1)S(1)}, bf16[32,3,32,128]{3,2,1,0:T(8,128)(2,1)S(1)}, u32[]{:S(2)}, u32[]{:S(2)}) collective-permute-start(bf16[32,3,32,128]{3,2,1,0:T(8,128)(2,1)S(1)} %far_upper.1), channel_id=1, source_target_pairs={{0,1},{1,2},{2,3},{3,4},{4,5},{5,6},{6,7},{7,8},{8,9},{9,10},{10,1... | collective-permute-start | bytes 2359304 | tf_op jit(solution)/shard_map/ppermute | solution.py:351
  44.8 24.9 %collective-permute-start.1 = (bf16[128,4096]{1,0:T(8,128)(2,1)}, bf16[128,4096]{1,0:T(8,128)(2,1)S(1)}, u32[]{:S(2)}, u32[]{:S(2)}) collective-permute-start(bf16[128,4096]{1,0:T(8,128)(2,1)} %get-tuple-element.26), channel_id=1, source_target_pairs={{1,0},{2,1},{3,2},{4,3},{5,4},{6,5},{7,6},{8,7},{9,8},{10,9},{11,1... | collective-permute-start | bytes 3145736 | tf_op jit(solution)/shard_map/ppermute | solution.py:307
  50.7 19.5 %collective-permute-start.2 = (bf16[128,4096]{1,0:T(8,128)(2,1)}, bf16[128,4096]{1,0:T(8,128)(2,1)S(1)}, u32[]{:S(2)}, u32[]{:S(2)}) collective-permute-start(bf16[128,4096]{1,0:T(8,128)(2,1)} %get-tuple-element.25), channel_id=1, source_target_pairs={{0,1},{1,2},{2,3},{3,4},{4,5},{5,6},{6,7},{7,8},{8,9},{9,10},{10,1... | collective-permute-start | bytes 3145736 | tf_op jit(solution)/shard_map/ppermute | solution.py:308
  66.2 53.7 %all-to-all-start.1 = ((bf16[32,4,32,128]{3,2,1,0:T(8,128)(2,1)}), bf16[32,4,32,128]{3,2,1,0:T(8,128)(2,1)S(1)}, u32[]{:S(2)}, u32[]{:S(2)}) async-start(bf16[32,4,32,128]{3,2,1,0:T(8,128)(2,1)} %pad_maximum_fusion), calls=%async_computation.1 | async-start | bytes 2097152 | tf_op jit(solution)/shard_map/all_to_all | solution.py:348
  70.2 2.2 %copy-start.1 = (bf16[256,64,128]{2,1,0:T(8,128)(2,1)S(1)}, bf16[256,64,128]{2,1,0:T(8,128)(2,1)}, u32[]{:S(2)}) copy-start(bf16[256,64,128]{2,1,0:T(8,128)(2,1)} %copy-done) | copy-start | bytes 12582916
  72.4 2.2 %copy-start.3 = (bf16[128,2,2,32,128]{4,3,2,1,0:T(8,128)(2,1)S(1)}, bf16[128,2,2,32,128]{4,3,2,1,0:T(8,128)(2,1)}, u32[]{:S(2)}) copy-start(bf16[128,2,2,32,128]{4,3,2,1,0:T(8,128)(2,1)} %copy-done.2) | copy-start | bytes 12582916
  90.6 28.1 %collective-permute-start.3 = (bf16[32,3,32,128]{3,2,1,0:T(8,128)(2,1)S(1)}, bf16[32,3,32,128]{3,2,1,0:T(8,128)(2,1)S(1)}, u32[]{:S(2)}, u32[]{:S(2)}) collective-permute-start(bf16[32,3,32,128]{3,2,1,0:T(8,128)(2,1)S(1)} %near_upper.1), channel_id=1, source_target_pairs={{0,1},{1,2},{2,3},{3,4},{4,5},{5,6},{6,7},{7,8},{8,9},{9,10},{10,1... | collective-permute-start | bytes 2359304 | tf_op jit(solution)/shard_map/ppermute | solution.py:359
  119.9 3.6 %copy-start.6 = (bf16[32,4,32,128]{3,2,1,0:T(8,128)(2,1)}, bf16[32,4,32,128]{3,2,1,0:T(8,128)(2,1)S(1)}, u32[]{:S(2)}) copy-start(bf16[32,4,32,128]{3,2,1,0:T(8,128)(2,1)S(1)} %all-to-all-done.1.in_ref) | copy-start | bytes 3145732
  119.9 24.5 %all-to-all-start = ((bf16[32,3,32,128]{3,2,1,0:T(8,128)(2,1)}), bf16[32,3,32,128]{3,2,1,0:T(8,128)(2,1)S(1)}, u32[]{:S(2)}, u32[]{:S(2)}) async-start(bf16[32,3,32,128]{3,2,1,0:T(8,128)(2,1)} %add_convert_fusion), calls=%async_computation | async-start | bytes 1572864 | tf_op jit(solution)/shard_map/all_to_all | solution.py:348
  144.4 0.9 copy-start.7

commit v4 on v3

--- a/solution.py
+++ b/solution.py
@@ -306,7 +306,6 @@
     plane1 = p_blocks[PLANE:]
     after = lax.ppermute(plane0, axes, down)
     before = lax.ppermute(plane1, axes, up)
-    after, before = lax.optimization_barrier((after, before))
 
     depth = 2 * position + lax.broadcasted_iota(jnp.int32, (2, PY, PX), 0)
     ypos = lax.broadcasted_iota(jnp.int32, (2, PY, PX), 1)
@@ -343,6 +342,7 @@
 
     near, far, prel, plhs = aligned(jnp.transpose(a_blocks, (1, 0, 2)), p_blocks, chosen.reshape(-1))
     scal = (scalars(0), scalars(1))
+    after, before, far = lax.optimization_barrier((after, before, far))
 
     def exchanged(rows):
         return lax.all_to_all(rows, "slab", split_axis=0, concat_axis=0, tiled=True)

time: 149 us -> 140 us (0.940)
  starting transfers between devices: 24.8 us -> 16 us
    ppermute x2, starting transfers between devices: 11.8 us -> 0.1 us  [per_device(): arrived = lax.ppermute(upper, axes, up)]
    all_to_all x2, starting transfers between devices: 7.14 us -> 9.49 us  [exchanged(): return lax.all_to_all(rows, 'slab', split_axis=0, concat_axis=0, tiled=True)]
    slice x1, local copies, waits for them, and re-layouts: 1.54 us -> 3.23 us  [per_device(): plane1 = p_blocks[PLANE:]]
    unnamed x16, local copies, waits for them, and re-layouts: 8.92 us -> 7.33 us
  transfers between devices with their start and end apart: 6 -> 6, of which waited for: 2 -> 2; matrix products, arithmetic and copies ran while one was open for 3% -> 6% of each run, Pallas kernels for 34% -> 49%
where the time goes in v4:
time: 140 us; the launch traced here: 139 us
  Pallas kernels  84.4 us (60%)
  waiting for transfers between devices  17.6 us (13%)
  starting transfers between devices  16 us (11%)
  local copies, waits for them, and re-layouts  15.7 us (11%)
  other arithmetic  4.69 us (3%)
    pallas_call x4, Pallas kernels, layer_part(): pl.pallas_call(kernel, out_shape=jax.ShapeDtypeStruct((AXY, 3, HALF, WIDE...  60.8 us
    pallas_call x1, Pallas kernels, aligned(): pl.pallas_call(align_kernel, out_shape=(jax.ShapeDtypeStruct((NEAR, count...  17.1 us
    all_to_all x2, waiting for transfers between devices, exchanged(): return lax.all_to_all(rows, 'slab', split_axis=0, concat_axis=0, tiled=True)  16.7 us
    all_to_all x2, starting transfers between devices, exchanged(): return lax.all_to_all(rows, 'slab', split_axis=0, concat_axis=0, tiled=True)  9.49 us
    unnamed x16, local copies, waits for them, and re-layouts  7.33 us
    pallas_call x2, Pallas kernels, flattened(): pl.pallas_call(flat_kernel, out_shape=jax.ShapeDtypeStruct((KC, rows, fla...  6.49 us
    ppermute x1, starting transfers between devices, per_device(): after = lax.ppermute(plane0, axes, down)  5.92 us
    slice x1, local copies, waits for them, and re-layouts, per_device(): plane1 = p_blocks[PLANE:]  3.23 us
  transfers between devices with their start and end apart: 6, of which 2 were waited for; matrix products, arithmetic and copies ran while one was open for 6% of the time, Pallas kernels for 49%

profile of v4, /device:TPU:0, one launch (start us, length us, event | category | flops | bytes accessed | tf_op | source)
XLA Modules:
  0.0 138.7 jit_solution(3859840238264746740)
XLA Ops:
  0.0 3.2 %fusion.14 = (bf16[128,4096]{1,0:T(8,128)(2,1)}, bf16[128,4096]{1,0:T(8,128)(2,1)}) fusion(bf16[256,4096]{1,0:T(8,128)(2,1)} %p_ref.1), kind=kLoop, calls=%fused_computation.91 | loop fusion | bytes 4194304 | tf_op jit(solution)/shard_map/slice | solution.py:306
  3.2 0.5 collective-permute-start.1
  3.7 5.9 %collective-permute-start = (bf16[128,4096]{1,0:T(8,128)(2,1)}, bf16[128,4096]{1,0:T(8,128)(2,1)}, u32[]{:S(2)}, u32[]{:S(2)}) collective-permute-start(bf16[128,4096]{1,0:T(8,128)(2,1)} %get-tuple-element.28), channel_id=1, source_target_pairs={{1,0},{2,1},{3,2},{4,3},{5,4},{6,5},{7,6},{8,7},{9,8},{10,9},{11,1... | collective-permute-start | bytes 3145736 | tf_op jit(solution)/shard_map/ppermute | solution.py:307
  9.9 0.1 and.183
  10.0 0.1 and.178
  10.2 0.1 and.181
  10.3 0.1 and.176
  10.5 0.1 and.174
  10.6 0.1 iota.274
  10.7 0.1 iota.256
  10.8 0.1 iota.248
  10.9 0.1 iota.290
  11.2 0.1 iota.262
  11.4 0.1 slice_reduce_fusion
  11.6 0.1 iota.271
  11.7 0.1 iota.265
  11.9 0.1 iota.244
  12.1 0.1 iota.235
  12.3 0.1 iota.232
  12.4 0.1 select_add_fusion.1
  12.6 0.1 slice.82
  12.7 0.1 slice.86
  12.7 0.1 slice.84
  13.2 0.1 copy.11
  13.4 0.2 reshape.1007.scal
  13.6 17.1 %align_blocks.1 = (bf16[5,256,32,128]{3,2,1,0:T(8,128)(2,1)}, bf16[2,256,32,128]{3,2,1,0:T(8,128)(2,1)S(1)}, bf16[256,64,128]{2,1,0:T(8,128)(2,1)S(1)}, bf16[128,2,2,32,128]{4,3,2,1,0:T(8,128)(2,1)S(1)}) custom-call(s32[1792]{0:T(1024)S(1)} %reshape.1007.scal, bf16[7,256,4096]{2,1,0:T(8,128)(2,1)} %bitcast.16, bf16[256,4096]{1,0:T(8,128)(2,1)S(1)} %copy-done.4), custom_call_target="tpu_custom_call" | custom-call | bytes 36700160 | tf_op jit(solution)/shard_map/align_blocks/pallas_call | solution.py:63
  30.7 2.1 %copy-done.2 = bf16[128,2,2,32,128]{4,3,2,1,0:T(8,128)(2,1)} copy-done((bf16[128,2,2,32,128]{4,3,2,1,0:T(8,128)(2,1)}, bf16[128,2,2,32,128]{4,3,2,1,0:T(8,128)(2,1)S(1)}, u32[]{:S(2)}) %copy-start.2) | copy-done | bytes 4194328
  32.8 0.8 dynamic-slice_bitcast_fusion.1
  33.5 1.1 fusion.17
  34.7 0.1 select_reduce_fusion
  34.8 1.3 compare_convert_fusion.1
  36.2 13.7 %far_upper.1 = bf16[32,3,32,128]{3,2,1,0:T(8,128)(2,1)S(1)} custom-call(s32[80]{0:T(128)S(1)} %get-tuple-element.23.scal, bf16[2,256,32,128]{3,2,1,0:T(8,128)(2,1)S(1)} %get-tuple-element.15.blocks, bf16[256,64,128]{2,1,0:T(8,128)(2,1)S(1)} %get-tuple-element.16.p_own.p_out, bf16[256,64,128]{2,1,0:T(8,128)(2,1)S(1)} %get-tuple-element.16.p_own.p_out, ...), custom_call_target="tpu_custom_call" | custom-call | flops 4294967296 | bytes 2097152 | tf_op jit(solution)/shard_map/far_upper/pallas_call | solution.py:247
  50.0 0.1 select_reduce_fusion.1
  50.2 13.9 %far_lower.1 = f32[32,3,32,128]{3,2,1,0:T(8,128)S(1)} custom-call(s32[80]{0:T(128)S(1)} %pad_add_fusion.scal, bf16[2,256,32,128]{3,2,1,0:T(8,128)(2,1)S(1)} %get-tuple-element.15.blocks, bf16[256,64,128]{2,1,0:T(8,128)(2,1)S(1)} %get-tuple-element.16.p_own.p_out, bf16[256,64,128]{2,1,0:T(8,128)(2,1)S(1)} %get-tuple-element.16.p_own.p_out, ...), custom_call_target="tpu_custom_call" | custom-call | flops 4294967296 | bytes 2097152 | tf_op jit(solution)/shard_map/far_lower/pallas_call | solution.py:247
  64.1 0.9 collective-permute-done.2
  65.0 0.2 fusion
  65.3 1.1 pad_maximum_fusion
  66.3 3.6 %all-to-all-start.1 = ((bf16[32,4,32,128]{3,2,1,0:T(8,128)(2,1)}), bf16[32,4,32,128]{3,2,1,0:T(8,128)(2,1)S(1)}, u32[]{:S(2)}, u32[]{:S(2)}) async-start(bf16[32,4,32,128]{3,2,1,0:T(8,128)(2,1)} %pad_maximum_fusion), calls=%async_computation.1 | async-start | bytes 2097152 | tf_op jit(solution)/shard_map/all_to_all | solution.py:348
  69.9 2.2 %copy-done.1 = bf16[256,64,128]{2,1,0:T(8,128)(2,1)S(1)} copy-done((bf16[256,64,128]{2,1,0:T(8,128)(2,1)S(1)}, bf16[256,64,128]{2,1,0:T(8,128)(2,1)}, u32[]{:S(2)}) %copy-start.1) | copy-done | bytes 4194328
  72.1 2.2 %copy-done.3 = bf16[128,2,2,32,128]{4,3,2,1,0:T(8,128)(2,1)S(1)} copy-done((bf16[128,2,2,32,128]{4,3,2,1,0:T(8,128)(2,1)S(1)}, bf16[128,2,2,32,128]{4,3,2,1,0:T(8,128)(2,1)}, u32[]{:S(2)}) %copy-start.3) | copy-done | bytes 4194328
  74.3 16.3 %near_upper.1 = bf16[32,3,32,128]{3,2,1,0:T(8,128)(2,1)S(1)} custom-call(s32[80]{0:T(128)S(1)} %get-tuple-element.23.scal, bf16[5,256,32,128]{3,2,1,0:T(8,128)(2,1)} %get-tuple-element.19.blocks, bf16[256,64,128]{2,1,0:T(8,128)(2,1)S(1)} %copy-done.1, bf16[128,4096]{1,0:T(8,128)(2,1)} %collective-permute-done.zin_ref, bf16[128,2,2,32,128]{4,3,2,1,0:T(8,128)(2,1)S(1)} %copy-done.3), custom_call_target="tpu_custom_call" | custom-call | flops 10737418240 | bytes 5242880 | tf_op jit(solution)/shard_map/near_upper/pallas_call | solution.py:247
  90.7 16.8 %near_lower.1 = f32[32,3,32,128]{3,2,1,0:T(8,128)S(1)} custom-call(s32[80]{0:T(128)S(1)} %pad_add_fusion.scal, bf16[5,256,32,128]{3,2,1,0:T(8,128)(2,1)} %get-tuple-element.19.blocks, bf16[256,64,128]{2,1,0:T(8,128)(2,1)S(1)} %copy-done.1, bf16[128,4096]{1,0:T(8,128)(2,1)S(1)} %collective-permute-done.1.zin_ref, bf16[128,2,2,32,128]{4,3,2,1,0:T(8,128)(2,1)} %copy-done.2), custom_call_target="tpu_custom_call" | custom-call | flops 10737418240 | bytes 5242880 | tf_op jit(solution)/shard_map/near_lower/pallas_call | solution.py:247
  107.6 1.2 add_convert_fusion
  108.7 5.9 %all-to-all-start = ((bf16[32,3,32,128]{3,2,1,0:T(8,128)(2,1)}), bf16[32,3,32,128]{3,2,1,0:T(8,128)(2,1)S(1)}, u32[]{:S(2)}, u32[]{:S(2)}) async-start(bf16[32,3,32,128]{3,2,1,0:T(8,128)(2,1)} %add_convert_fusion), calls=%async_computation | async-start | bytes 1572864 | tf_op jit(solution)/shard_map/all_to_all | solution.py:348
  114.7 3.5 %flatten_far.1.refs_0_ = bf16[7,32,4096]{2,1,0:T(8,128)(2,1)} custom-call(bf16[32,4,32,128]{3,2,1,0:T(8,128)(2,1)} %copy-done.5), custom_call_target="tpu_custom_call" | custom-call | tf_op jit(solution)/shard_map/flatten_far/pallas_call | solution.py:285
  118.2 16.7 %all-to-all-done.in_ref = bf16[32,3,32,128]{3,2,1,0:T(8,128)(2,1)S(1)} async-done(((bf16[32,3,32,128]{3,2,1,0:T(8,128)(2,1)}), bf16[32,3,32,128]{3,2,1,0:T(8,128)(2,1)S(1)}, u32[]{:S(2)}, u32[]{:S(2)}) %all-to-all-start) | async-done | bytes 786464 | tf_op jit(solution)/shard_map/all_to_all | solution.py:348
  134.9 0.9 copy-done.6
  135.8 3.0 %flatten_near.1 = bf16[7,32,4096]{2,1,0:T(8,128)(2,1)} custom-call(bf16[32,3,32,128]{3,2,1,0:T(8,128)(2,1)} %copy-done.6, bf16[7,32,4096]{2,1,0:T(8,128)(2,1)} %flatten_far.1.refs_0_), custom_call_target="tpu_custom_call", output_to_operand_aliasing={{}: (1, {})} | custom-call | tf_op jit(solution)/shard_map/flatten_near/pallas_call | solution.py:285
  (74 shorter events, 1.9 us)
Async XLA Ops:
  0.0 13.6 %copy-start.4 = (bf16[256,4096]{1,0:T(8,128)(2,1)S(1)}, bf16[256,4096]{1,0:T(8,128)(2,1)}, u32[]{:S(2)}) copy-start(bf16[256,4096]{1,0:T(8,128)(2,1)} %p_ref.1) | copy-start | bytes 6291460
  0.0 11.3 %slice-start = ((s32[256]{0:T(256)}), s32[128]{0:T(128)S(1)}, s32[]{:S(2)}) async-start(s32[256]{0:T(256)} %param.8), calls=%async_computation.2 | async-start | bytes 1024 | tf_op jit(solution)/shard_map/slice | solution.py:331
  0.0 13.2 %copy-start.7 = (s32[256,7]{0,1:T(8,128)S(1)}, s32[256,7]{0,1:T(8,128)}, u32[]{:S(2)}) copy-start(s32[256,7]{0,1:T(8,128)} %param.6) | copy-start | bytes 21508
  3.2 33.0 %collective-permute-start.1 = (bf16[128,4096]{1,0:T(8,128)(2,1)}, bf16[128,4096]{1,0:T(8,128)(2,1)S(1)}, u32[]{:S(2)}, u32[]{:S(2)}) collective-permute-start(bf16[128,4096]{1,0:T(8,128)(2,1)} %get-tuple-element.27), channel_id=1, source_target_pairs={{0,1},{1,2},{2,3},{3,4},{4,5},{5,6},{6,7},{7,8},{8,9},{9,10},{10,1... | collective-permute-start | bytes 3145736 | tf_op jit(solution)/shard_map/ppermute | solution.py:308
  3.7 32.6 %collective-permute-start = (bf16[128,4096]{1,0:T(8,128)(2,1)}, bf16[128,4096]{1,0:T(8,128)(2,1)}, u32[]{:S(2)}, u32[]{:S(2)}) collective-permute-start(bf16[128,4096]{1,0:T(8,128)(2,1)} %get-tuple-element.28), channel_id=1, source_target_pairs={{1,0},{2,1},{3,2},{4,3},{5,4},{6,5},{7,6},{8,7},{9,8},{10,9},{11,1... | collective-permute-start | bytes 3145736 | tf_op jit(solution)/shard_map/ppermute | solution.py:307
  30.7 2.1 %copy-start.2 = (bf16[128,2,2,32,128]{4,3,2,1,0:T(8,128)(2,1)}, bf16[128,2,2,32,128]{4,3,2,1,0:T(8,128)(2,1)S(1)}, u32[]{:S(2)}) copy-start(bf16[128,2,2,32,128]{4,3,2,1,0:T(8,128)(2,1)S(1)} %get-tuple-element.17.plhs) | copy-start | bytes 12582916
  32.8 17.5 %copy-start = (bf16[256,64,128]{2,1,0:T(8,128)(2,1)}, bf16[256,64,128]{2,1,0:T(8,128)(2,1)S(1)}, u32[]{:S(2)}) copy-start(bf16[256,64,128]{2,1,0:T(8,128)(2,1)S(1)} %get-tuple-element.16.p_own.p_out) | copy-start | bytes 12582916
  50.0 15.0 %collective-permute-start.2 = (bf16[32,3,32,128]{3,2,1,0:T(8,128)(2,1)S(1)}, bf16[32,3,32,128]{3,2,1,0:T(8,128)(2,1)S(1)}, u32[]{:S(2)}, u32[]{:S(2)}) collective-permute-start(bf16[32,3,32,128]{3,2,1,0:T(8,128)(2,1)S(1)} %far_upper.1), channel_id=1, source_target_pairs={{0,1},{1,2},{2,3},{3,4},{4,5},{5,6},{6,7},{7,8},{8,9},{9,10},{10,1... | collective-permute-start | bytes 2359304 | tf_op jit(solution)/shard_map/ppermute | solution.py:351
  66.3 42.4 %all-to-all-start.1 = ((bf16[32,4,32,128]{3,2,1,0:T(8,128)(2,1)}), bf16[32,4,32,128]{3,2,1,0:T(8,128)(2,1)S(1)}, u32[]{:S(2)}, u32[]{:S(2)}) async-start(bf16[32,4,32,128]{3,2,1,0:T(8,128)(2,1)} %pad_maximum_fusion), calls=%async_computation.1 | async-start | bytes 2097152 | tf_op jit(solution)/shard_map/all_to_all | solution.py:348
  69.9 2.2 %copy-start.1 = (bf16[256,64,128]{2,1,0:T(8,128)(2,1)S(1)}, bf16[256,64,128]{2,1,0:T(8,128)(2,1)}, u32[]{:S(2)}) copy-start(bf16[256,64,128]{2,1,0:T(8,128)(2,1)} %copy-done) | copy-start | bytes 12582916
  72.1 2.2 %copy-start.3 = (bf16[128,2,2,32,128]{4,3,2,1,0:T(8,128)(2,1)S(1)}, bf16[128,2,2,32,128]{4,3,2,1,0:T(8,128)(2,1)}, u32[]{:S(2)}) copy-start(bf16[128,2,2,32,128]{4,3,2,1,0:T(8,128)(2,1)} %copy-done.2) | copy-start | bytes 12582916
  90.6 16.9 %collective-permute-start.3 = (bf16[32,3,32,128]{3,2,1,0:T(8,128)(2,1)S(1)}, bf16[32,3,32,128]{3,2,1,0:T(8,128)(2,1)S(1)}, u32[]{:S(2)}, u32[]{:S(2)}) collective-permute-start(bf16[32,3,32,128]{3,2,1,0:T(8,128)(2,1)S(1)} %near_upper.1), channel_id=1, source_target_pairs={{0,1},{1,2},{2,3},{3,4},{4,5},{5,6},{6,7},{7,8},{8,9},{9,10},{10,1... | collective-permute-start | bytes 2359304 | tf_op jit(solution)/shard_map/ppermute | solution.py:359
  108.7 5.9 %copy-start.5 = (bf16[32,4,32,128]{3,2,1,0:T(8,128)(2,1)}, bf16[32,4,32,128]{3,2,1,0:T(8,128)(2,1)S(1)}, u32[]{:S(2)}) copy-start(bf16[32,4,32,128]{3,2,1,0:T(8,128)(2,1)S(1)} %all-to-all-done.1.in_ref) | copy-start | bytes 3145732
  108.7 26.1 %all-to-all-start = ((bf16[32,3,32,128]{3,2,1,0:T(8,128)(2,1)}), bf16[32,3,32,128]{3,2,1,0:T(8,128)(2,1)S(1)}, u32[]{:S(2)}, u32[]{:S(2)}) async-start(bf16[32,3,32,128]{3,2,1,0:T(8,128)(2,1)} %add_convert_fusion), calls=%async_computation | async-start | bytes 1572864 | tf_op jit(solution)/shard_map/all_to_all | solution.py:348
  134.9 0.9 copy-start.6

commit v5 on v4

--- a/solution.py
+++ b/solution.py
@@ -86,7 +86,7 @@
                 pltpu.VMEM((rows, BS, WIDE), F32),
             ],
         ),
-        compiler_params=pltpu.CompilerParams(vmem_limit_bytes=32 * 1024 * 1024),
+        compiler_params=pltpu.CompilerParams(vmem_limit_bytes=16 * 1024 * 1024),
         cost_estimate=pl.CostEstimate(
             flops=0, bytes_accessed=5 * KC * count * flat, transcendentals=0
         ),
@@ -259,7 +259,7 @@
             out_specs=pl.BlockSpec((AXY, 3, HALF, WIDE), lambda s, _: (0, 0, 0, 0)),
             scratch_shapes=scratch + [pltpu.VMEM((AXY, 2, BS, WIDE), F32)],
         ),
-        compiler_params=pltpu.CompilerParams(vmem_limit_bytes=44 * 1024 * 1024),
+        compiler_params=pltpu.CompilerParams(vmem_limit_bytes=(28 if zin is None else 37) * 1024 * 1024),
         cost_estimate=pl.CostEstimate(
             flops=PLANE * count * 64 * BS**3,
             bytes_accessed=PLANE * count * flat * 2,

time: 140 us -> 137 us (0.979)
  Pallas kernels: 84.4 us -> 78.3 us
  local copies, waits for them, and re-layouts: 15.7 us -> 17.6 us
    pallas_call x4, Pallas kernels: 60.8 us -> 56.9 us  [layer_part(): pl.pallas_call(kernel, out_shape=jax.ShapeDtypeStruct((AXY, 3, HALF, WIDE...]
    pallas_call x1, Pallas kernels: 17.1 us -> 14.9 us  [aligned(): pl.pallas_call(align_kernel, out_shape=(jax.ShapeDtypeStruct((NEAR, count...]
    unnamed x16 -> x18, local copies, waits for them, and re-layouts: 7.33 us -> 9.28 us
    ppermute x2, waiting for transfers between devices: 0.89 us -> 2.51 us  [per_device(): arrived = lax.ppermute(upper, axes, up)]
    all_to_all x2, waiting for transfers between devices: 16.7 us -> 15.1 us  [exchanged(): return lax.all_to_all(rows, 'slab', split_axis=0, concat_axis=0, tiled=True)]
  transfers between devices with their start and end apart: 6 -> 6, of which waited for: 2 -> 2; matrix products, arithmetic and copies ran while one was open for 6% -> 6% of each run, Pallas kernels for 49% -> 47%
where the time goes in v5:
time: 137 us; the launch traced here: 135 us
  Pallas kernels  78.3 us (57%)
  waiting for transfers between devices  17.7 us (13%)
  local copies, waits for them, and re-layouts  17.6 us (13%)
  starting transfers between devices  16 us (12%)
  other arithmetic  4.65 us (3%)
    pallas_call x4, Pallas kernels, layer_part(): pl.pallas_call(kernel, out_shape=jax.ShapeDtypeStruct((AXY, 3, HALF, WIDE...  56.9 us
    all_to_all x2, waiting for transfers between devices, exchanged(): return lax.all_to_all(rows, 'slab', split_axis=0, concat_axis=0, tiled=True)  15.1 us
    pallas_call x1, Pallas kernels, aligned(): pl.pallas_call(align_kernel, out_shape=(jax.ShapeDtypeStruct((NEAR, count...  14.9 us
    all_to_all x2, starting transfers between devices, exchanged(): return lax.all_to_all(rows, 'slab', split_axis=0, concat_axis=0, tiled=True)  9.49 us
    unnamed x18, local copies, waits for them, and re-layouts  9.28 us
    pallas_call x2, Pallas kernels, flattened(): pl.pallas_call(flat_kernel, out_shape=jax.ShapeDtypeStruct((KC, rows, fla...  6.49 us
    ppermute x1, starting transfers between devices, per_device(): after = lax.ppermute(plane0, axes, down)  5.92 us
    slice x1, local copies, waits for them, and re-layouts, per_device(): plane1 = p_blocks[PLANE:]  3.24 us
  transfers between devices with their start and end apart: 6, of which 2 were waited for; matrix products, arithmetic and copies ran while one was open for 6% of the time, Pallas kernels for 47%

profile of v5, /device:TPU:0, one launch (start us, length us, event | category | flops | bytes accessed | tf_op | source)
XLA Modules:
  0.0 134.6 jit_solution(8049568481707834444)
XLA Ops:
  0.0 3.2 %fusion.14 = (bf16[128,4096]{1,0:T(8,128)(2,1)}, bf16[128,4096]{1,0:T(8,128)(2,1)}) fusion(bf16[256,4096]{1,0:T(8,128)(2,1)} %p_ref.1), kind=kLoop, calls=%fused_computation.91 | loop fusion | bytes 4194304 | tf_op jit(solution)/shard_map/slice | solution.py:306
  3.2 0.5 collective-permute-start.1
  3.7 5.9 %collective-permute-start = (bf16[128,4096]{1,0:T(8,128)(2,1)}, bf16[128,4096]{1,0:T(8,128)(2,1)}, u32[]{:S(2)}, u32[]{:S(2)}) collective-permute-start(bf16[128,4096]{1,0:T(8,128)(2,1)} %get-tuple-element.28), channel_id=1, source_target_pairs={{1,0},{2,1},{3,2},{4,3},{5,4},{6,5},{7,6},{8,7},{9,8},{10,9},{11,1... | collective-permute-start | bytes 3145736 | tf_op jit(solution)/shard_map/ppermute | solution.py:307
  9.9 0.1 and.183
  10.0 0.1 and.178
  10.2 0.1 and.181
  10.3 0.1 and.176
  10.5 0.1 and.174
  10.6 0.1 iota.274
  10.7 0.1 iota.256
  10.8 0.1 iota.248
  10.9 0.1 iota.290
  11.2 0.1 iota.262
  11.4 0.1 slice_reduce_fusion
  11.6 0.1 iota.271
  11.8 0.1 iota.265
  11.9 0.1 iota.244
  12.1 0.1 iota.235
  12.3 0.1 iota.232
  12.4 0.1 select_add_fusion.1
  12.6 0.1 slice.82
  12.7 0.1 slice.86
  12.8 0.1 slice.84
  13.3 0.1 copy.11
  13.4 0.2 reshape.1007.scal
  13.6 14.9 %align_blocks.1 = (bf16[5,256,32,128]{3,2,1,0:T(8,128)(2,1)S(1)}, bf16[2,256,32,128]{3,2,1,0:T(8,128)(2,1)S(1)}, bf16[256,64,128]{2,1,0:T(8,128)(2,1)S(1)}, bf16[128,2,2,32,128]{4,3,2,1,0:T(8,128)(2,1)S(1)}) custom-call(s32[1792]{0:T(1024)S(1)} %reshape.1007.scal, bf16[7,256,4096]{2,1,0:T(8,128)(2,1)} %bitcast.16, bf16[256,4096]{1,0:T(8,128)(2,1)S(1)} %copy-done.4), custom_call_target="tpu_custom_call" | custom-call | bytes 36700160 | tf_op jit(solution)/shard_map/align_blocks/pallas_call | solution.py:63
  28.6 4.0 %copy-done.5 = bf16[5,256,32,128]{3,2,1,0:T(8,128)(2,1)} copy-done((bf16[5,256,32,128]{3,2,1,0:T(8,128)(2,1)}, bf16[5,256,32,128]{3,2,1,0:T(8,128)(2,1)S(1)}, u32[]{:S(2)}) %copy-start.5) | copy-done | bytes 10485784
  32.6 0.8 dynamic-slice_bitcast_fusion.1
  33.3 1.1 fusion.17
  34.4 0.1 select_reduce_fusion
  34.6 1.3 compare_convert_fusion.1
  36.0 12.1 %far_upper.1 = bf16[32,3,32,128]{3,2,1,0:T(8,128)(2,1)S(1)} custom-call(s32[80]{0:T(128)S(1)} %get-tuple-element.23.scal, bf16[2,256,32,128]{3,2,1,0:T(8,128)(2,1)S(1)} %get-tuple-element.15.blocks, bf16[256,64,128]{2,1,0:T(8,128)(2,1)S(1)} %get-tuple-element.16.p_own.p_out, bf16[256,64,128]{2,1,0:T(8,128)(2,1)S(1)} %get-tuple-element.16.p_own.p_out, ...), custom_call_target="tpu_custom_call" | custom-call | flops 4294967296 | bytes 2097152 | tf_op jit(solution)/shard_map/far_upper/pallas_call | solution.py:247
  48.1 0.1 select_reduce_fusion.1
  48.3 12.2 %far_lower.1 = f32[32,3,32,128]{3,2,1,0:T(8,128)S(1)} custom-call(s32[80]{0:T(128)S(1)} %pad_add_fusion.scal, bf16[2,256,32,128]{3,2,1,0:T(8,128)(2,1)S(1)} %get-tuple-element.15.blocks, bf16[256,64,128]{2,1,0:T(8,128)(2,1)S(1)} %get-tuple-element.16.p_own.p_out, bf16[256,64,128]{2,1,0:T(8,128)(2,1)S(1)} %get-tuple-element.16.p_own.p_out, ...), custom_call_target="tpu_custom_call" | custom-call | flops 4294967296 | bytes 2097152 | tf_op jit(solution)/shard_map/far_lower/pallas_call | solution.py:247
  60.6 2.5 %collective-permute-done.2 = bf16[32,3,32,128]{3,2,1,0:T(8,128)(2,1)S(1)} collective-permute-done((bf16[32,3,32,128]{3,2,1,0:T(8,128)(2,1)S(1)}, bf16[32,3,32,128]{3,2,1,0:T(8,128)(2,1)S(1)}, u32[]{:S(2)}, u32[]{:S(2)}) %collective-permute-start.2) | collective-permute-done | bytes 786464 | tf_op jit(solution)/shard_map/ppermute | solution.py:351
  63.1 0.2 fusion
  63.4 1.1 pad_maximum_fusion
  64.4 3.6 %all-to-all-start.1 = ((bf16[32,4,32,128]{3,2,1,0:T(8,128)(2,1)}), bf16[32,4,32,128]{3,2,1,0:T(8,128)(2,1)S(1)}, u32[]{:S(2)}, u32[]{:S(2)}) async-start(bf16[32,4,32,128]{3,2,1,0:T(8,128)(2,1)} %pad_maximum_fusion), calls=%async_computation.1 | async-start | bytes 2097152 | tf_op jit(solution)/shard_map/all_to_all | solution.py:348
  68.0 2.2 %copy-done.1 = bf16[256,64,128]{2,1,0:T(8,128)(2,1)S(1)} copy-done((bf16[256,64,128]{2,1,0:T(8,128)(2,1)S(1)}, bf16[256,64,128]{2,1,0:T(8,128)(2,1)}, u32[]{:S(2)}) %copy-start.1) | copy-done | bytes 4194328
  70.2 2.2 %copy-done.3 = bf16[128,2,2,32,128]{4,3,2,1,0:T(8,128)(2,1)S(1)} copy-done((bf16[128,2,2,32,128]{4,3,2,1,0:T(8,128)(2,1)S(1)}, bf16[128,2,2,32,128]{4,3,2,1,0:T(8,128)(2,1)}, u32[]{:S(2)}) %copy-start.3) | copy-done | bytes 4194328
  72.4 16.3 %near_upper.1 = bf16[32,3,32,128]{3,2,1,0:T(8,128)(2,1)S(1)} custom-call(s32[80]{0:T(128)S(1)} %get-tuple-element.23.scal, bf16[5,256,32,128]{3,2,1,0:T(8,128)(2,1)} %copy-done.5, bf16[256,64,128]{2,1,0:T(8,128)(2,1)S(1)} %copy-done.1, bf16[128,4096]{1,0:T(8,128)(2,1)} %collective-permute-done.zin_ref, bf16[128,2,2,32,128]{4,3,2,1,0:T(8,128)(2,1)S(1)} %copy-done.3), custom_call_target="tpu_custom_call" | custom-call | flops 10737418240 | bytes 5242880 | tf_op jit(solution)/shard_map/near_upper/pallas_call | solution.py:247
  88.8 16.2 %near_lower.1 = f32[32,3,32,128]{3,2,1,0:T(8,128)S(1)} custom-call(s32[80]{0:T(128)S(1)} %pad_add_fusion.scal, bf16[5,256,32,128]{3,2,1,0:T(8,128)(2,1)} %copy-done.5, bf16[256,64,128]{2,1,0:T(8,128)(2,1)S(1)} %copy-done.1, bf16[128,4096]{1,0:T(8,128)(2,1)S(1)} %collective-permute-done.1.zin_ref, bf16[128,2,2,32,128]{4,3,2,1,0:T(8,128)(2,1)S(1)} %copy-done.3), custom_call_target="tpu_custom_call" | custom-call | flops 10737418240 | bytes 5242880 | tf_op jit(solution)/shard_map/near_lower/pallas_call | solution.py:247
  105.0 1.2 add_convert_fusion
  106.2 5.9 %all-to-all-start = ((bf16[32,3,32,128]{3,2,1,0:T(8,128)(2,1)}), bf16[32,3,32,128]{3,2,1,0:T(8,128)(2,1)S(1)}, u32[]{:S(2)}, u32[]{:S(2)}) async-start(bf16[32,3,32,128]{3,2,1,0:T(8,128)(2,1)} %add_convert_fusion), calls=%async_computation | async-start | bytes 1572864 | tf_op jit(solution)/shard_map/all_to_all | solution.py:348
  112.1 3.5 %flatten_far.1.refs_0_ = bf16[7,32,4096]{2,1,0:T(8,128)(2,1)} custom-call(bf16[32,4,32,128]{3,2,1,0:T(8,128)(2,1)} %copy-done.6), custom_call_target="tpu_custom_call" | custom-call | tf_op jit(solution)/shard_map/flatten_far/pallas_call | solution.py:285
  115.6 15.1 %all-to-all-done.in_ref = bf16[32,3,32,128]{3,2,1,0:T(8,128)(2,1)S(1)} async-done(((bf16[32,3,32,128]{3,2,1,0:T(8,128)(2,1)}), bf16[32,3,32,128]{3,2,1,0:T(8,128)(2,1)S(1)}, u32[]{:S(2)}, u32[]{:S(2)}) %all-to-all-start) | async-done | bytes 786464 | tf_op jit(solution)/shard_map/all_to_all | solution.py:348
  130.8 0.9 copy-done.7
  131.7 3.0 %flatten_near.1 = bf16[7,32,4096]{2,1,0:T(8,128)(2,1)} custom-call(bf16[32,3,32,128]{3,2,1,0:T(8,128)(2,1)} %copy-done.7, bf16[7,32,4096]{2,1,0:T(8,128)(2,1)} %flatten_far.1.refs_0_), custom_call_target="tpu_custom_call", output_to_operand_aliasing={{}: (1, {})} | custom-call | tf_op jit(solution)/shard_map/flatten_near/pallas_call | solution.py:285
  (76 shorter events, 1.9 us)
Async XLA Ops:
  0.0 13.6 %copy-start.4 = (bf16[256,4096]{1,0:T(8,128)(2,1)S(1)}, bf16[256,4096]{1,0:T(8,128)(2,1)}, u32[]{:S(2)}) copy-start(bf16[256,4096]{1,0:T(8,128)(2,1)} %p_ref.1) | copy-start | bytes 6291460
  0.0 11.3 %slice-start = ((s32[256]{0:T(256)}), s32[128]{0:T(128)S(1)}, s32[]{:S(2)}) async-start(s32[256]{0:T(256)} %param.8), calls=%async_computation.2 | async-start | bytes 1024 | tf_op jit(solution)/shard_map/slice | solution.py:331
  0.0 13.2 %copy-start.8 = (s32[256,7]{0,1:T(8,128)S(1)}, s32[256,7]{0,1:T(8,128)}, u32[]{:S(2)}) copy-start(s32[256,7]{0,1:T(8,128)} %param.6) | copy-start | bytes 21508
  3.2 32.7 %collective-permute-start.1 = (bf16[128,4096]{1,0:T(8,128)(2,1)}, bf16[128,4096]{1,0:T(8,128)(2,1)S(1)}, u32[]{:S(2)}, u32[]{:S(2)}) collective-permute-start(bf16[128,4096]{1,0:T(8,128)(2,1)} %get-tuple-element.27), channel_id=1, source_target_pairs={{0,1},{1,2},{2,3},{3,4},{4,5},{5,6},{6,7},{7,8},{8,9},{9,10},{10,1... | collective-permute-start | bytes 3145736 | tf_op jit(solution)/shard_map/ppermute | solution.py:308
  3.7 32.3 %collective-permute-start = (bf16[128,4096]{1,0:T(8,128)(2,1)}, bf16[128,4096]{1,0:T(8,128)(2,1)}, u32[]{:S(2)}, u32[]{:S(2)}) collective-permute-start(bf16[128,4096]{1,0:T(8,128)(2,1)} %get-tuple-element.28), channel_id=1, source_target_pairs={{1,0},{2,1},{3,2},{4,3},{5,4},{6,5},{7,6},{8,7},{9,8},{10,9},{11,1... | collective-permute-start | bytes 3145736 | tf_op jit(solution)/shard_map/ppermute | solution.py:307
  28.5 4.0 %copy-start.5 = (bf16[5,256,32,128]{3,2,1,0:T(8,128)(2,1)}, bf16[5,256,32,128]{3,2,1,0:T(8,128)(2,1)S(1)}, u32[]{:S(2)}) copy-start(bf16[5,256,32,128]{3,2,1,0:T(8,128)(2,1)S(1)} %get-tuple-element.19.blocks) | copy-start | bytes 31457284
  32.6 15.8 %copy-start = (bf16[256,64,128]{2,1,0:T(8,128)(2,1)}, bf16[256,64,128]{2,1,0:T(8,128)(2,1)S(1)}, u32[]{:S(2)}) copy-start(bf16[256,64,128]{2,1,0:T(8,128)(2,1)S(1)} %get-tuple-element.16.p_own.p_out) | copy-start | bytes 12582916
  32.6 15.8 %copy-start.2 = (bf16[128,2,2,32,128]{4,3,2,1,0:T(8,128)(2,1)}, bf16[128,2,2,32,128]{4,3,2,1,0:T(8,128)(2,1)S(1)}, u32[]{:S(2)}) copy-start(bf16[128,2,2,32,128]{4,3,2,1,0:T(8,128)(2,1)S(1)} %get-tuple-element.17.plhs) | copy-start | bytes 12582916
  48.1 15.0 %collective-permute-start.2 = (bf16[32,3,32,128]{3,2,1,0:T(8,128)(2,1)S(1)}, bf16[32,3,32,128]{3,2,1,0:T(8,128)(2,1)S(1)}, u32[]{:S(2)}, u32[]{:S(2)}) collective-permute-start(bf16[32,3,32,128]{3,2,1,0:T(8,128)(2,1)S(1)} %far_upper.1), channel_id=1, source_target_pairs={{0,1},{1,2},{2,3},{3,4},{4,5},{5,6},{6,7},{7,8},{8,9},{9,10},{10,1... | collective-permute-start | bytes 2359304 | tf_op jit(solution)/shard_map/ppermute | solution.py:351
  64.4 41.7 %all-to-all-start.1 = ((bf16[32,4,32,128]{3,2,1,0:T(8,128)(2,1)}), bf16[32,4,32,128]{3,2,1,0:T(8,128)(2,1)S(1)}, u32[]{:S(2)}, u32[]{:S(2)}) async-start(bf16[32,4,32,128]{3,2,1,0:T(8,128)(2,1)} %pad_maximum_fusion), calls=%async_computation.1 | async-start | bytes 2097152 | tf_op jit(solution)/shard_map/all_to_all | solution.py:348
  68.0 2.2 %copy-start.1 = (bf16[256,64,128]{2,1,0:T(8,128)(2,1)S(1)}, bf16[256,64,128]{2,1,0:T(8,128)(2,1)}, u32[]{:S(2)}) copy-start(bf16[256,64,128]{2,1,0:T(8,128)(2,1)} %copy-done) | copy-start | bytes 12582916
  70.2 2.2 %copy-start.3 = (bf16[128,2,2,32,128]{4,3,2,1,0:T(8,128)(2,1)S(1)}, bf16[128,2,2,32,128]{4,3,2,1,0:T(8,128)(2,1)}, u32[]{:S(2)}) copy-start(bf16[128,2,2,32,128]{4,3,2,1,0:T(8,128)(2,1)} %copy-done.2) | copy-start | bytes 12582916
  88.7 16.2 %collective-permute-start.3 = (bf16[32,3,32,128]{3,2,1,0:T(8,128)(2,1)S(1)}, bf16[32,3,32,128]{3,2,1,0:T(8,128)(2,1)S(1)}, u32[]{:S(2)}, u32[]{:S(2)}) collective-permute-start(bf16[32,3,32,128]{3,2,1,0:T(8,128)(2,1)S(1)} %near_upper.1), channel_id=1, source_target_pairs={{0,1},{1,2},{2,3},{3,4},{4,5},{5,6},{6,7},{7,8},{8,9},{9,10},{10,1... | collective-permute-start | bytes 2359304 | tf_op jit(solution)/shard_map/ppermute | solution.py:359
  106.2 5.9 %copy-start.6 = (bf16[32,4,32,128]{3,2,1,0:T(8,128)(2,1)}, bf16[32,4,32,128]{3,2,1,0:T(8,128)(2,1)S(1)}, u32[]{:S(2)}) copy-start(bf16[32,4,32,128]{3,2,1,0:T(8,128)(2,1)S(1)} %all-to-all-done.1.in_ref) | copy-start | bytes 3145732
  106.2 24.6 %all-to-all-start = ((bf16[32,3,32,128]{3,2,1,0:T(8,128)(2,1)}), bf16[32,3,32,128]{3,2,1,0:T(8,128)(2,1)S(1)}, u32[]{:S(2)}, u32[]{:S(2)}) async-start(bf16[32,3,32,128]{3,2,1,0:T(8,128)(2,1)} %add_convert_fusion), calls=%async_computation | async-start | bytes 1572864 | tf_op jit(solution)/shard_map/all_to_all | solution.py:348
  130.8 0.9 copy-start.7
